TPU v7x, 128 devices: a whole 4x4x4 slice. The times are simulated.
128 devices in a mesh: seq: 32 (over y, x, core), seqs: 4 (over z).
Axes of the slice: x: 4, y: 4, z: 4, core: 2. Of those that a mesh axis runs over, the one named last changes fastest.
Arguments:
- queries: float32 [524288, 2, 128], P(('seqs', 'seq')), parts along dimension 0, may hold values from -0.09375 to 0.09375
- key_vectors: float32 [524288, 2, 128], P(('seqs', 'seq')), parts along dimension 0, may hold values from -0.09375 to 0.09375
- value_vectors: float32 [524288, 2, 128], P(('seqs', 'seq')), parts along dimension 0, may hold values from -0.09375 to 0.09375
- grad_output: float32 [524288, 2, 128], P(('seqs', 'seq')), parts along dimension 0, may hold values from -6 to 6
Outputs:
- grad_queries: float32 [524288, 2, 128], P(('seqs', 'seq')), parts along dimension 0
- grad_keys: float32 [524288, 2, 128], P(('seqs', 'seq')), parts along dimension 0
- grad_values: float32 [524288, 2, 128], P(('seqs', 'seq')), parts along dimension 0
There are 4 independent parts, one for each index of `seqs`. A program takes and returns all parts, laid end to end along the dimension named above; each array names one. Nothing has to cross between parts.
All inputs are finite; a program needn't handle non-finite values.
Results may differ from a plain program's by a relative error of at most 0.0001.
Values sent between devices are 32-bit elements; how exact they have to be, the bound alone decides.
No kernel may reach another device: no remote copies, remote signals or barrier semaphores. Data moves between devices by JAX's collectives and lax.ppermute only.
A program may use at most 192 MiB of HBM per device.

v0:
```python
import functools

import jax
import jax.numpy as jnp
from jax import lax
from jax.experimental import pallas as pl
from jax.experimental.pallas import tpu as pltpu
from jax.sharding import PartitionSpec as P

HEAD = 128
HEADS = 2
CHUNK = 128
SLICES = 4

BF16 = jnp.bfloat16
F32 = jnp.float32
NAT = (((1,), (0,)), ((), ()))
ROWS = (((1,), (1,)), ((), ()))
COLS = (((0,), (0,)), ((), ()))
MIB = 1024 * 1024


def mm(a, b, dims=NAT):
    return lax.dot_general(a, b, dims, preferred_element_type=F32)


def parts(x):
    hi = x.astype(BF16)
    lo = (x - hi.astype(F32)).astype(BF16)
    return hi, lo


def pair(x):
    return jnp.concatenate(parts(x), axis=1)


def stacked(xx):
    hi, lo = xx[:, :HEAD], xx[:, HEAD:]
    top = jnp.concatenate([hi, hi], axis=1)
    low = jnp.concatenate([lo, lo], axis=1)
    return jnp.concatenate([top, low], axis=0)


def halves(x):
    return x[:, :HEAD] + x[:, HEAD:]


def quads(x):
    return x[:CHUNK, :HEAD] + x[:CHUNK, HEAD:] + x[CHUNK:, :HEAD]


def states_kernel(tile, q, k, v, g, qs, ks, vs, gs, pt, sg, sgt, own_p, own_s, kb, vb, qb, gb, sems):
    tokens = q.shape[0] // HEADS
    steps = tokens // tile
    rows = tile * HEADS

    def fetch(step, slot):
        back = steps - 1 - step
        out = []
        for j, (src, dst, at) in enumerate(((k, kb, step), (v, vb, step), (q, qb, back), (g, gb, back))):
            out.append(pltpu.make_async_copy(src.at[pl.ds(at * rows, rows)], dst.at[slot], sems.at[j, slot]))
        return out

    for c in fetch(0, 0):
        c.start()
    own_p[...] = jnp.zeros_like(own_p)
    own_s[...] = jnp.zeros_like(own_s)
    per = tile // CHUNK

    def body(step, carry):
        slot = lax.rem(step, 2)

        @pl.when(step + 1 < steps)
        def _():
            for c in fetch(step + 1, 1 - slot):
                c.start()

        for c in fetch(step, slot):
            c.wait()
        back = steps - 1 - step
        for c in range(per):
            r = per - 1 - c
            for h in range(HEADS):
                tok = pl.ds(pl.multiple_of(step * tile + c * CHUNK, CHUNK), CHUNK)
                inside = pl.ds(c * CHUNK * HEADS + h, CHUNK, HEADS)
                kk = pair(kb[slot, inside, :])
                vv = pair(vb[slot, inside, :])
                ks[h, tok, :] = kk
                vs[h, tok, :] = vv
                p = own_p[h]
                pt[step * per + c, h] = pair(p)
                own_p[h] = p + quads(mm(vv, kk, COLS))

                tok = pl.ds(pl.multiple_of(back * tile + r * CHUNK, CHUNK), CHUNK)
                inside = pl.ds(r * CHUNK * HEADS + h, CHUNK, HEADS)
                qq = pair(qb[slot, inside, :])
                gg = pair(gb[slot, inside, :])
                qs[h, tok, :] = qq
                gs[h, tok, :] = gg
                s = own_s[h]
                sg[back * per + r, h] = pair(s)
                sgt[back * per + r, h] = pair(s.T)
                own_s[h] = s + quads(mm(qq, gg, COLS))
        return carry

    lax.fori_loop(0, steps, body, 0)


def inside_kernel(first, count, unroll, qs, ks, vs, gs, pt, sg, sgt, dq, dk, dv):
    at_row = lax.broadcasted_iota(jnp.int32, (CHUNK, CHUNK), 0)
    at_col = lax.broadcasted_iota(jnp.int32, (CHUNK, CHUNK), 1)
    upper = at_row <= at_col
    lower = at_row >= at_col

    def one(n, h):
        tok = pl.ds(pl.multiple_of((first + n) * CHUNK, CHUNK), CHUNK)
        out = pl.ds(pl.multiple_of(n * CHUNK, CHUNK), CHUNK)
        qq, kk, vv, gg = (x[h, tok, :] for x in (qs, ks, vs, gs))

        def finish(score, keep, left, right, state):
            hi, lo = parts(jnp.where(keep, halves(score), 0.0))
            top = jnp.concatenate([hi, left[:, :HEAD]], axis=1)
            low = jnp.concatenate([lo, left[:, HEAD:]], axis=1)
            lhs = jnp.concatenate([top, low], axis=0)
            return quads(mm(lhs, jnp.concatenate([right, state], axis=0)))

        dq[h, out, :] = finish(mm(gg, stacked(vv), ROWS), lower, gg, kk, pt[first + n, h])
        dk[h, out, :] = finish(mm(vv, stacked(gg), ROWS), upper, vv, qq, sgt[first + n, h])
        dv[h, out, :] = finish(mm(kk, stacked(qq), ROWS), upper, kk, gg, sg[first + n, h])

    def body(i, carry):
        for u in range(unroll):
            for h in range(HEADS):
                one(i * unroll + u, h)
        return carry

    lax.fori_loop(0, count // unroll, body, 0)


def outside_kernel(tile, slices, ks, vs, gs, before, after, *rest):
    partial = rest[: 3 * slices]
    outs = rest[3 * slices : 3 * slices + 3]
    ob, sems = rest[3 * slices + 3 :]
    tokens = ks.shape[1]
    steps = tokens // tile
    rows = tile * HEADS
    span = tokens // slices
    weights = []
    for h in range(HEADS):
        b = pair(before[h])
        a = pair(after[h])
        weights.append((jnp.concatenate([b, b], axis=0), stacked(a), jnp.concatenate([a, a], axis=0)))

    def send(j, step, slot):
        return pltpu.make_async_copy(ob.at[j, slot], outs[j].at[pl.ds(step * rows, rows)], sems.at[j, slot])

    for step in range(steps):
        slot = step % 2
        base = step * tile
        part, off = base // span, base % span
        for j, (src, dims) in enumerate(((gs, NAT), (vs, ROWS), (ks, NAT))):
            if step >= 2:
                send(j, step - 2, slot).wait()
            for h in range(HEADS):
                x = halves(mm(src[h, base : base + tile, :], weights[h][j], dims))
                ob[j, slot, pl.ds(h, tile, HEADS), :] = x + partial[part * 3 + j][h, off : off + tile, :]
            send(j, step, slot).start()
    for step in range(max(steps - 2, 0), steps):
        for j in range(3):
            send(j, step, step % 2).wait()


VM = pl.BlockSpec(memory_space=pltpu.VMEM)
ANY = pl.BlockSpec(memory_space=pl.ANY)


def vmem(*arrays):
    return [pltpu.with_memory_space_constraint(a, pltpu.VMEM) for a in arrays]


def body(shape, queries, key_vectors, value_vectors, grad_output):
    tokens = queries.shape[0]
    chunks = tokens // CHUNK
    flat = [x.reshape(tokens * HEADS, HEAD) for x in (queries, key_vectors, value_vectors, grad_output)]

    tile = 512
    split_shape = pltpu.VMEM((HEADS, tokens, 2 * HEAD), BF16)
    state_shape = pltpu.VMEM((chunks, HEADS, HEAD, 2 * HEAD), BF16)
    own_shape = pltpu.VMEM((HEADS, HEAD, HEAD), F32)
    *split, pt, sg, sgt, own_p, own_s = pl.pallas_call(
        functools.partial(states_kernel, tile),
        out_shape=[split_shape] * 4 + [state_shape] * 3 + [own_shape] * 2,
        in_specs=[ANY] * 4,
        out_specs=[VM] * 9,
        scratch_shapes=[pltpu.VMEM((2, tile * HEADS, HEAD), F32)] * 4 + [pltpu.SemaphoreType.DMA((4, 2))],
        compiler_params=pltpu.CompilerParams(vmem_limit_bytes=8 * MIB),
        cost_estimate=pl.CostEstimate(flops=10**9, bytes_accessed=16 * MIB, transcendentals=0),
        name="states",
    )(*flat)

    core = lax.axis_index("seq") % 2
    mine = jnp.where(core == 0, own_p, own_s)
    other = jnp.where(core == 0, own_s, own_p)
    devices = lax.axis_size("seq")
    here = lax.axis_index("seq")
    sibling = [(i, i ^ 1) for i in range(devices)]
    total = mine + lax.ppermute(other, "seq", sibling)
    entered = jnp.zeros_like(total)

    count = chunks // SLICES
    partial = []

    def inside(at, after):
        fed = vmem(*split, pt, sg, sgt)
        return pl.pallas_call(
            functools.partial(inside_kernel, at * count, count, 1),
            out_shape=[pltpu.VMEM((HEADS, tokens // SLICES, HEAD), F32)] * 3,
            in_specs=[VM] * 7,
            out_specs=[VM] * 3,
            compiler_params=pltpu.CompilerParams(vmem_limit_bytes=8 * MIB),
            cost_estimate=pl.CostEstimate(flops=3 * 10**9, bytes_accessed=MIB, transcendentals=0),
            name="inside" + str(at),
        )(*fed)

    step = 2
    at = 0
    while step < devices:
        got = lax.ppermute(total, "seq", [(i, i ^ step) for i in range(devices)])
        partial += inside(at, None)
        at += 1
        partner_first = ((here & step) != 0) == (core == 0)
        entered = entered + jnp.where(partner_first, got, 0.0)
        total = total + got
        step *= 2
    while at < SLICES:
        partial += inside(at, None)
        at += 1
    got = lax.ppermute(entered + mine, "seq", sibling)
    before = jnp.where(core == 0, entered, got)
    after = jnp.where(core == 0, got, entered)

    tile = 256
    out = pl.pallas_call(
        functools.partial(outside_kernel, tile, SLICES),
        out_shape=[jax.ShapeDtypeStruct((tokens * HEADS, HEAD), F32)] * 3,
        in_specs=[VM] * (5 + 3 * SLICES),
        out_specs=[ANY] * 3,
        scratch_shapes=[pltpu.VMEM((3, 2, tile * HEADS, HEAD), F32), pltpu.SemaphoreType.DMA((3, 2))],
        compiler_params=pltpu.CompilerParams(vmem_limit_bytes=8 * MIB),
        cost_estimate=pl.CostEstimate(flops=10**9, bytes_accessed=12 * MIB, transcendentals=0),
        name="outside",
    )(*vmem(split[1], split[2], split[3], before, after, *partial))
    return tuple(x.reshape(queries.shape) for x in out)


def solution(mesh):
    spec = P(("seqs", "seq"), None, None)
    return jax.shard_map(
        functools.partial(body, dict(mesh.shape)),
        mesh=mesh,
        in_specs=(spec,) * 4,
        out_specs=(spec,) * 3,
        check_vma=False,
    )
```

profile of v0, /device:TPU:1, one launch (start us, length us, event | category | flops | bytes accessed | tf_op | source)
XLA Modules:
  0.0 118.0 jit_solution(5175227250175751987)
XLA Ops:
  0.7 2.2 %copy-done.20 = f32[4096,2,128]{2,1,0:T(2,128)S(1)} copy-done((f32[4096,2,128]{2,1,0:T(2,128)S(1)}, f32[4096,2,128]{2,1,0:T(2,128)}, u32[]{:S(2)}) %copy-start.20) | copy-done | bytes 4194328
  2.8 2.2 %copy-done.21 = f32[4096,2,128]{2,1,0:T(2,128)S(1)} copy-done((f32[4096,2,128]{2,1,0:T(2,128)S(1)}, f32[4096,2,128]{2,1,0:T(2,128)}, u32[]{:S(2)}) %copy-start.21) | copy-done | bytes 4194328
  5.0 2.2 %copy-done.22 = f32[4096,2,128]{2,1,0:T(2,128)S(1)} copy-done((f32[4096,2,128]{2,1,0:T(2,128)S(1)}, f32[4096,2,128]{2,1,0:T(2,128)}, u32[]{:S(2)}) %copy-start.22) | copy-done | bytes 4194328
  7.2 2.2 %copy-done.23 = f32[4096,2,128]{2,1,0:T(2,128)S(1)} copy-done((f32[4096,2,128]{2,1,0:T(2,128)S(1)}, f32[4096,2,128]{2,1,0:T(2,128)}, u32[]{:S(2)}) %copy-start.23) | copy-done | bytes 4194328
  9.4 8.1 %states.1 = (bf16[2,4096,256]{2,1,0:T(8,128)(2,1)S(1)}, bf16[2,4096,256]{2,1,0:T(8,128)(2,1)S(1)}, bf16[2,4096,256]{2,1,0:T(8,128)(2,1)S(1)}, bf16[2,4096,256]{2...) custom-call(f32[8192,128]{1,0:T(8,128)S(1)} %bitcast.7, ...), custom_call_target="tpu_custom_call" | custom-call | flops 1000000000 | bytes 16777216 | tf_op jit(solution)/shard_map/states/pallas_call | solution.py:190
  17.5 2.0 %copy-done.6 = bf16[2,4096,256]{2,1,0:T(8,128)(2,1)} copy-done((bf16[2,4096,256]{2,1,0:T(8,128)(2,1)}, bf16[2,4096,256]{2,1,0:T(8,128)(2,1)S(1)}, u32[]{:S(2)}) %copy-start.6) | copy-done | bytes 4194328
  19.5 2.0 %copy-done.10 = bf16[2,4096,256]{2,1,0:T(8,128)(2,1)} copy-done((bf16[2,4096,256]{2,1,0:T(8,128)(2,1)}, bf16[2,4096,256]{2,1,0:T(8,128)(2,1)S(1)}, u32[]{:S(2)}) %copy-start.10) | copy-done | bytes 4194328
  21.5 1.5 %collective-permute-start = (f32[2,128,128]{2,1,0:T(8,128)S(1)}, f32[2,128,128]{2,1,0:T(8,128)S(1)}, u32[]{:S(2)}, u32[]{:S(2)}) collective-permute-start(f32[2,128,128]{2,1,0:T(8,128)S(1)} %broadcast_select_fusion.2), channel_id=1, source_target_pairs={{0,4},{4,0},{8,12},{12,8},{16,20},{20,16},{24,28},{28,24},{32,36},... | collective-permute-start | bytes 393224 | tf_op jit(solution)/shard_map/ppermute | solution.py:207
  23.0 1.0 collective-permute-done
  24.0 1.4 %collective-permute-start.1 = (f32[2,128,128]{2,1,0:T(8,128)S(1)}, f32[2,128,128]{2,1,0:T(8,128)S(1)}, u32[]{:S(2)}, u32[]{:S(2)}) collective-permute-start(f32[2,128,128]{2,1,0:T(8,128)S(1)} %fusion.1), channel_id=1, source_target_pairs={{0,8},{4,12},{8,0},{12,4},{16,24},{20,28},{24,16},{28,20},{32,40},... | collective-permute-start | bytes 393224 | tf_op jit(solution)/shard_map/ppermute | solution.py:228
  25.4 3.4 %collective-permute-done.1 = f32[2,128,128]{2,1,0:T(8,128)S(1)} collective-permute-done((f32[2,128,128]{2,1,0:T(8,128)S(1)}, f32[2,128,128]{2,1,0:T(8,128)S(1)}, u32[]{:S(2)}, u32[]{:S(2)}) %collective-permute-start.1) | collective-permute-done | bytes 131104 | tf_op jit(solution)/shard_map/ppermute | solution.py:228
  28.8 2.9 %collective-permute-start.2 = (f32[2,128,128]{2,1,0:T(8,128)S(1)}, f32[2,128,128]{2,1,0:T(8,128)S(1)}, u32[]{:S(2)}, u32[]{:S(2)}) collective-permute-start(f32[2,128,128]{2,1,0:T(8,128)S(1)} %add.30), channel_id=1, source_target_pairs={{0,16},{4,20},{8,24},{12,28},{16,0},{20,4},{24,8},{28,12},{32,48},... | collective-permute-start | bytes 393224 | tf_op jit(solution)/shard_map/ppermute | solution.py:228
  31.7 2.2 %copy-done.7 = bf16[2,4096,256]{2,1,0:T(8,128)(2,1)S(1)} copy-done((bf16[2,4096,256]{2,1,0:T(8,128)(2,1)S(1)}, bf16[2,4096,256]{2,1,0:T(8,128)(2,1)}, u32[]{:S(2)}) %copy-start.7) | copy-done | bytes 4194328
  33.9 2.2 %copy-done.11 = bf16[2,4096,256]{2,1,0:T(8,128)(2,1)S(1)} copy-done((bf16[2,4096,256]{2,1,0:T(8,128)(2,1)S(1)}, bf16[2,4096,256]{2,1,0:T(8,128)(2,1)}, u32[]{:S(2)}) %copy-start.11) | copy-done | bytes 4194328
  36.1 10.4 %inside3.1 = (f32[2,1024,128]{2,1,0:T(8,128)S(1)}, f32[2,1024,128]{2,1,0:T(8,128)S(1)}, f32[2,1024,128]{2,1,0:T(8,128)S(1)}) custom-call(bf16[2,4096,256]{2,1,0:T(8,128)(2,1)S(1)} %copy-done.11, bf16[2,4096,256]{2,1,0:T(8,128)(2,1)S(1)} %get-tuple-element.27.ks, bf16[2,4096,256]{2,1,0:T(8,128)(2,1)S(1)} %get-tuple-element.28.vs, ...), custom_call_target="tpu_custom_call" | custom-call | flops 3000000000 | bytes 1048576 | tf_op jit(solution)/shard_map/inside3/pallas_call | solution.py:215
  46.5 1.4 %collective-permute-start.3 = (f32[2,128,128]{2,1,0:T(8,128)S(1)}, f32[2,128,128]{2,1,0:T(8,128)S(1)}, u32[]{:S(2)}, u32[]{:S(2)}) collective-permute-start(f32[2,128,128]{2,1,0:T(8,128)S(1)} %add.32), channel_id=1, source_target_pairs={{0,32},{4,36},{8,40},{12,44},{16,48},{20,52},{24,56},{28,60},{32,0... | collective-permute-start | bytes 393224 | tf_op jit(solution)/shard_map/ppermute | solution.py:228
  47.9 10.4 %inside2.1 = (f32[2,1024,128]{2,1,0:T(8,128)S(1)}, f32[2,1024,128]{2,1,0:T(8,128)S(1)}, f32[2,1024,128]{2,1,0:T(8,128)S(1)}) custom-call(bf16[2,4096,256]{2,1,0:T(8,128)(2,1)S(1)} %copy-done.12, bf16[2,4096,256]{2,1,0:T(8,128)(2,1)S(1)} %get-tuple-element.27.ks, bf16[2,4096,256]{2,1,0:T(8,128)(2,1)S(1)} %get-tuple-element.28.vs, ...), custom_call_target="tpu_custom_call" | custom-call | flops 3000000000 | bytes 1048576 | tf_op jit(solution)/shard_map/inside2/pallas_call | solution.py:215
  59.3 1.0 copy-done.26
  62.0 2.6 %collective-permute-start.4 = (f32[2,128,128]{2,1,0:T(8,128)}, f32[2,128,128]{2,1,0:T(8,128)}, u32[]{:S(2)}, u32[]{:S(2)}) collective-permute-start(f32[2,128,128]{2,1,0:T(8,128)} %add.34), channel_id=1, source_target_pairs={{0,64},{4,68},{8,72},{12,76},{16,80},{20,84},{24,88},{28,92},{32,9... | collective-permute-start | bytes 393224 | tf_op jit(solution)/shard_map/ppermute | solution.py:228
  64.6 10.4 %inside1.1 = (f32[2,1024,128]{2,1,0:T(8,128)S(1)}, f32[2,1024,128]{2,1,0:T(8,128)S(1)}, f32[2,1024,128]{2,1,0:T(8,128)S(1)}) custom-call(bf16[2,4096,256]{2,1,0:T(8,128)(2,1)S(1)} %copy-done.12, bf16[2,4096,256]{2,1,0:T(8,128)(2,1)S(1)} %get-tuple-element.27.ks, bf16[2,4096,256]{2,1,0:T(8,128)(2,1)S(1)} %get-tuple-element.28.vs, ...), custom_call_target="tpu_custom_call" | custom-call | flops 3000000000 | bytes 1048576 | tf_op jit(solution)/shard_map/inside1/pallas_call | solution.py:215
  76.0 1.0 copy-done.32
  78.0 1.1 fusion
  79.1 1.1 collective-permute-start.5
  80.1 2.2 %copy-done.1 = bf16[2,4096,256]{2,1,0:T(8,128)(2,1)S(1)} copy-done((bf16[2,4096,256]{2,1,0:T(8,128)(2,1)S(1)}, bf16[2,4096,256]{2,1,0:T(8,128)(2,1)}, u32[]{:S(2)}) %copy-start.1) | copy-done | bytes 4194328
  82.3 2.2 %copy-done.4 = bf16[2,4096,256]{2,1,0:T(8,128)(2,1)S(1)} copy-done((bf16[2,4096,256]{2,1,0:T(8,128)(2,1)S(1)}, bf16[2,4096,256]{2,1,0:T(8,128)(2,1)}, u32[]{:S(2)}) %copy-start.4) | copy-done | bytes 4194328
  84.5 2.2 %copy-done.8 = bf16[2,4096,256]{2,1,0:T(8,128)(2,1)S(1)} copy-done((bf16[2,4096,256]{2,1,0:T(8,128)(2,1)S(1)}, bf16[2,4096,256]{2,1,0:T(8,128)(2,1)}, u32[]{:S(2)}) %copy-start.8) | copy-done | bytes 4194328
  86.7 2.2 %copy-done.13 = bf16[2,4096,256]{2,1,0:T(8,128)(2,1)S(1)} copy-done((bf16[2,4096,256]{2,1,0:T(8,128)(2,1)S(1)}, bf16[2,4096,256]{2,1,0:T(8,128)(2,1)}, u32[]{:S(2)}) %copy-start.13) | copy-done | bytes 4194328
  88.9 2.2 %copy-done.15 = bf16[32,2,128,256]{3,2,1,0:T(8,128)(2,1)S(1)} copy-done((bf16[32,2,128,256]{3,2,1,0:T(8,128)(2,1)S(1)}, bf16[32,2,128,256]{3,2,1,0:T(8,128)(2,1)}, u32[]{:S(2)}) %copy-start.15) | copy-done | bytes 4194328
  91.1 2.2 %copy-done.17 = bf16[32,2,128,256]{3,2,1,0:T(8,128)(2,1)S(1)} copy-done((bf16[32,2,128,256]{3,2,1,0:T(8,128)(2,1)S(1)}, bf16[32,2,128,256]{3,2,1,0:T(8,128)(2,1)}, u32[]{:S(2)}) %copy-start.17) | copy-done | bytes 4194328
  93.3 2.2 %copy-done.19 = bf16[32,2,128,256]{3,2,1,0:T(8,128)(2,1)S(1)} copy-done((bf16[32,2,128,256]{3,2,1,0:T(8,128)(2,1)S(1)}, bf16[32,2,128,256]{3,2,1,0:T(8,128)(2,1)}, u32[]{:S(2)}) %copy-start.19) | copy-done | bytes 4194328
  95.5 10.4 %inside0.1 = (f32[2,1024,128]{2,1,0:T(8,128)S(1)}, f32[2,1024,128]{2,1,0:T(8,128)S(1)}, f32[2,1024,128]{2,1,0:T(8,128)S(1)}) custom-call(bf16[2,4096,256]{2,1,0:T(8,128)(2,1)S(1)} %copy-done.13, bf16[2,4096,256]{2,1,0:T(8,128)(2,1)S(1)} %copy-done.1, bf16[2,4096,256]{2,1,0:T(8,128)(2,1)S(1)} %copy-done.4, bf16[2,4096,256]{2,1,0:T(8,128)(2,1)S(1)} %copy-done.8, ...), custom_call_target="tpu_custom_call" | custom-call | flops 3000000000 | bytes 1048576 | tf_op jit(solution)/shard_map/inside0/pallas_call | solution.py:215
  106.0 11.9 %outside.1 = (f32[8192,128]{1,0:T(8,128)}, f32[8192,128]{1,0:T(8,128)}, f32[8192,128]{1,0:T(8,128)}) custom-call(bf16[2,4096,256]{2,1,0:T(8,128)(2,1)S(1)} %copy-done.2, bf16[2,4096,256]{2,1,0:T(8,128)(2,1)S(1)} %copy-done.5, bf16[2,4096,256]{2,1,0:T(8,128)(2,1)S(1)} %copy-done.9, f32[2,128,128]{2,1,0:T(8,128)S(1)} %get-tuple-element.54.before, ...), custom_call_target="tpu_custom_call" | custom-call | flops 1000000000 | bytes 12582912 | tf_op jit(solution)/shard_map/outside/pallas_call | solution.py:243
  (69 shorter events, 4.8 us)
Async XLA Ops:
  0.6 2.2 %copy-start.20 = (f32[4096,2,128]{2,1,0:T(2,128)S(1)}, f32[4096,2,128]{2,1,0:T(2,128)}, u32[]{:S(2)}) copy-start(f32[4096,2,128]{2,1,0:T(2,128)} %param.4) | copy-start | bytes 12582916
  2.8 2.2 %copy-start.21 = (f32[4096,2,128]{2,1,0:T(2,128)S(1)}, f32[4096,2,128]{2,1,0:T(2,128)}, u32[]{:S(2)}) copy-start(f32[4096,2,128]{2,1,0:T(2,128)} %param.5) | copy-start | bytes 12582916
  5.0 2.2 %copy-start.22 = (f32[4096,2,128]{2,1,0:T(2,128)S(1)}, f32[4096,2,128]{2,1,0:T(2,128)}, u32[]{:S(2)}) copy-start(f32[4096,2,128]{2,1,0:T(2,128)} %param.6) | copy-start | bytes 12582916
  7.2 2.2 %copy-start.23 = (f32[4096,2,128]{2,1,0:T(2,128)S(1)}, f32[4096,2,128]{2,1,0:T(2,128)}, u32[]{:S(2)}) copy-start(f32[4096,2,128]{2,1,0:T(2,128)} %param.7) | copy-start | bytes 12582916
  21.4 43.1 %copy-start = (bf16[2,4096,256]{2,1,0:T(8,128)(2,1)}, bf16[2,4096,256]{2,1,0:T(8,128)(2,1)S(1)}, u32[]{:S(2)}) copy-start(bf16[2,4096,256]{2,1,0:T(8,128)(2,1)S(1)} %get-tuple-element.27.ks) | copy-start | bytes 12582916
  21.5 43.1 %copy-start.3 = (bf16[2,4096,256]{2,1,0:T(8,128)(2,1)}, bf16[2,4096,256]{2,1,0:T(8,128)(2,1)S(1)}, u32[]{:S(2)}) copy-start(bf16[2,4096,256]{2,1,0:T(8,128)(2,1)S(1)} %get-tuple-element.28.vs) | copy-start | bytes 12582916
  21.5 43.1 %copy-start.14 = (bf16[32,2,128,256]{3,2,1,0:T(8,128)(2,1)}, bf16[32,2,128,256]{3,2,1,0:T(8,128)(2,1)S(1)}, u32[]{:S(2)}) copy-start(bf16[32,2,128,256]{3,2,1,0:T(8,128)(2,1)S(1)} %get-tuple-element.33.pt) | copy-start | bytes 12582916
  21.5 43.1 %copy-start.16 = (bf16[32,2,128,256]{3,2,1,0:T(8,128)(2,1)}, bf16[32,2,128,256]{3,2,1,0:T(8,128)(2,1)S(1)}, u32[]{:S(2)}) copy-start(bf16[32,2,128,256]{3,2,1,0:T(8,128)(2,1)S(1)} %get-tuple-element.34.sg) | copy-start | bytes 12582916
  21.5 43.1 %copy-start.18 = (bf16[32,2,128,256]{3,2,1,0:T(8,128)(2,1)}, bf16[32,2,128,256]{3,2,1,0:T(8,128)(2,1)S(1)}, u32[]{:S(2)}) copy-start(bf16[32,2,128,256]{3,2,1,0:T(8,128)(2,1)S(1)} %get-tuple-element.35.sgt) | copy-start | bytes 12582916
  21.5 2.5 %collective-permute-start = (f32[2,128,128]{2,1,0:T(8,128)S(1)}, f32[2,128,128]{2,1,0:T(8,128)S(1)}, u32[]{:S(2)}, u32[]{:S(2)}) collective-permute-start(f32[2,128,128]{2,1,0:T(8,128)S(1)} %broadcast_select_fusion.2), channel_id=1, source_target_pairs={{0,4},{4,0},{8,12},{12,8},{16,20},{20,16},{24,28},{28,24},{32,36},... | collective-permute-start | bytes 393224 | tf_op jit(solution)/shard_map/ppermute | solution.py:207
  24.0 4.8 %collective-permute-start.1 = (f32[2,128,128]{2,1,0:T(8,128)S(1)}, f32[2,128,128]{2,1,0:T(8,128)S(1)}, u32[]{:S(2)}, u32[]{:S(2)}) collective-permute-start(f32[2,128,128]{2,1,0:T(8,128)S(1)} %fusion.1), channel_id=1, source_target_pairs={{0,8},{4,12},{8,0},{12,4},{16,24},{20,28},{24,16},{28,20},{32,40},... | collective-permute-start | bytes 393224 | tf_op jit(solution)/shard_map/ppermute | solution.py:228
  28.8 17.7 %collective-permute-start.2 = (f32[2,128,128]{2,1,0:T(8,128)S(1)}, f32[2,128,128]{2,1,0:T(8,128)S(1)}, u32[]{:S(2)}, u32[]{:S(2)}) collective-permute-start(f32[2,128,128]{2,1,0:T(8,128)S(1)} %add.30), channel_id=1, source_target_pairs={{0,16},{4,20},{8,24},{12,28},{16,0},{20,4},{24,8},{28,12},{32,48},... | collective-permute-start | bytes 393224 | tf_op jit(solution)/shard_map/ppermute | solution.py:228
  36.1 11.8 %copy-start.12 = (bf16[2,4096,256]{2,1,0:T(8,128)(2,1)S(1)}, bf16[2,4096,256]{2,1,0:T(8,128)(2,1)}, u32[]{:S(2)}) copy-start(bf16[2,4096,256]{2,1,0:T(8,128)(2,1)} %copy-done.10) | copy-start | bytes 12582916
  46.5 11.8 %copy-start.36 = (f32[2,128,128]{2,1,0:T(8,128)}, f32[2,128,128]{2,1,0:T(8,128)S(1)}, u32[]{:S(2)}) copy-start(f32[2,128,128]{2,1,0:T(8,128)S(1)} %collective-permute-done.2) | copy-start | bytes 393220
  46.5 14.7 %collective-permute-start.3 = (f32[2,128,128]{2,1,0:T(8,128)S(1)}, f32[2,128,128]{2,1,0:T(8,128)S(1)}, u32[]{:S(2)}, u32[]{:S(2)}) collective-permute-start(f32[2,128,128]{2,1,0:T(8,128)S(1)} %add.32), channel_id=1, source_target_pairs={{0,32},{4,36},{8,40},{12,44},{16,48},{20,52},{24,56},{28,60},{32,0... | collective-permute-start | bytes 393224 | tf_op jit(solution)/shard_map/ppermute | solution.py:228
  62.0 16.0 %collective-permute-start.4 = (f32[2,128,128]{2,1,0:T(8,128)}, f32[2,128,128]{2,1,0:T(8,128)}, u32[]{:S(2)}, u32[]{:S(2)}) collective-permute-start(f32[2,128,128]{2,1,0:T(8,128)} %add.34), channel_id=1, source_target_pairs={{0,64},{4,68},{8,72},{12,76},{16,80},{20,84},{24,88},{28,92},{32,9... | collective-permute-start | bytes 393224 | tf_op jit(solution)/shard_map/ppermute | solution.py:228
  79.1 26.9 %collective-permute-start.5 = (f32[2,128,128]{2,1,0:T(8,128)S(1)}, f32[2,128,128]{2,1,0:T(8,128)S(1)}, u32[]{:S(2)}, u32[]{:S(2)}) collective-permute-start(f32[2,128,128]{2,1,0:T(8,128)S(1)} %get-tuple-element.51), channel_id=1, source_target_pairs={{0,4},{4,0},{8,12},{12,8},{16,20},{20,16},{24,28},{28,24},{32,36},... | collective-permute-start | bytes 393224 | tf_op jit(solution)/shard_map/ppermute | solution.py:238
  80.1 2.2 %copy-start.1 = (bf16[2,4096,256]{2,1,0:T(8,128)(2,1)S(1)}, bf16[2,4096,256]{2,1,0:T(8,128)(2,1)}, u32[]{:S(2)}) copy-start(bf16[2,4096,256]{2,1,0:T(8,128)(2,1)} %copy-done) | copy-start | bytes 12582916
  82.3 2.2 %copy-start.4 = (bf16[2,4096,256]{2,1,0:T(8,128)(2,1)S(1)}, bf16[2,4096,256]{2,1,0:T(8,128)(2,1)}, u32[]{:S(2)}) copy-start(bf16[2,4096,256]{2,1,0:T(8,128)(2,1)} %copy-done.3) | copy-start | bytes 12582916
  84.5 2.2 %copy-start.8 = (bf16[2,4096,256]{2,1,0:T(8,128)(2,1)S(1)}, bf16[2,4096,256]{2,1,0:T(8,128)(2,1)}, u32[]{:S(2)}) copy-start(bf16[2,4096,256]{2,1,0:T(8,128)(2,1)} %copy-done.6) | copy-start | bytes 12582916
  86.7 2.2 %copy-start.13 = (bf16[2,4096,256]{2,1,0:T(8,128)(2,1)S(1)}, bf16[2,4096,256]{2,1,0:T(8,128)(2,1)}, u32[]{:S(2)}) copy-start(bf16[2,4096,256]{2,1,0:T(8,128)(2,1)} %copy-done.10) | copy-start | bytes 12582916
  88.9 2.2 %copy-start.15 = (bf16[32,2,128,256]{3,2,1,0:T(8,128)(2,1)S(1)}, bf16[32,2,128,256]{3,2,1,0:T(8,128)(2,1)}, u32[]{:S(2)}) copy-start(bf16[32,2,128,256]{3,2,1,0:T(8,128)(2,1)} %copy-done.14) | copy-start | bytes 12582916
  91.1 2.2 %copy-start.17 = (bf16[32,2,128,256]{3,2,1,0:T(8,128)(2,1)S(1)}, bf16[32,2,128,256]{3,2,1,0:T(8,128)(2,1)}, u32[]{:S(2)}) copy-start(bf16[32,2,128,256]{3,2,1,0:T(8,128)(2,1)} %copy-done.16) | copy-start | bytes 12582916
  95.5 10.5 %copy-start.2 = (bf16[2,4096,256]{2,1,0:T(8,128)(2,1)S(1)}, bf16[2,4096,256]{2,1,0:T(8,128)(2,1)}, u32[]{:S(2)}) copy-start(bf16[2,4096,256]{2,1,0:T(8,128)(2,1)} %copy-done) | copy-start | bytes 12582916
  95.5 10.5 %copy-start.5 = (bf16[2,4096,256]{2,1,0:T(8,128)(2,1)S(1)}, bf16[2,4096,256]{2,1,0:T(8,128)(2,1)}, u32[]{:S(2)}) copy-start(bf16[2,4096,256]{2,1,0:T(8,128)(2,1)} %copy-done.3) | copy-start | bytes 12582916
  95.5 10.5 %copy-start.9 = (bf16[2,4096,256]{2,1,0:T(8,128)(2,1)S(1)}, bf16[2,4096,256]{2,1,0:T(8,128)(2,1)}, u32[]{:S(2)}) copy-start(bf16[2,4096,256]{2,1,0:T(8,128)(2,1)} %copy-done.6) | copy-start | bytes 12582916
  95.5 10.5 %copy-start.25 = (f32[2,1024,128]{2,1,0:T(8,128)S(1)}, f32[2,1024,128]{2,1,0:T(8,128)}, u32[]{:S(2)}) copy-start(f32[2,1024,128]{2,1,0:T(8,128)} %copy-done.24) | copy-start | bytes 3145732
  95.5 10.5 %copy-start.27 = (f32[2,1024,128]{2,1,0:T(8,128)S(1)}, f32[2,1024,128]{2,1,0:T(8,128)}, u32[]{:S(2)}) copy-start(f32[2,1024,128]{2,1,0:T(8,128)} %copy-done.26) | copy-start | bytes 3145732
  95.5 10.5 %copy-start.29 = (f32[2,1024,128]{2,1,0:T(8,128)S(1)}, f32[2,1024,128]{2,1,0:T(8,128)}, u32[]{:S(2)}) copy-start(f32[2,1024,128]{2,1,0:T(8,128)} %copy-done.28) | copy-start | bytes 3145732
  95.5 10.5 %copy-start.31 = (f32[2,1024,128]{2,1,0:T(8,128)S(1)}, f32[2,1024,128]{2,1,0:T(8,128)}, u32[]{:S(2)}) copy-start(f32[2,1024,128]{2,1,0:T(8,128)} %copy-done.30) | copy-start | bytes 3145732
  95.5 10.5 %copy-start.33 = (f32[2,1024,128]{2,1,0:T(8,128)S(1)}, f32[2,1024,128]{2,1,0:T(8,128)}, u32[]{:S(2)}) copy-start(f32[2,1024,128]{2,1,0:T(8,128)} %copy-done.32) | copy-start | bytes 3145732
  95.5 10.5 %copy-start.35 = (f32[2,1024,128]{2,1,0:T(8,128)S(1)}, f32[2,1024,128]{2,1,0:T(8,128)}, u32[]{:S(2)}) copy-start(f32[2,1024,128]{2,1,0:T(8,128)} %copy-done.34) | copy-start | bytes 3145732
  (12 other events, 17.1 us)
where the time goes:
time: 119 us; the launch traced here: 118 us
  Pallas kernels  61.5 us (52%)
  local copies, waits for them, and re-layouts  38.4 us (32%)
  starting transfers between devices  10.9 us (9%)
  waiting for transfers between devices  4.43 us (4%)
  other arithmetic  1.87 us (2%)
    pallas_call x4, Pallas kernels, inside(): pl.pallas_call(functools.partial(inside_kernel, at * count, count, 1), ou...  41.5 us
    unnamed x76, local copies, waits for them, and re-layouts  38.4 us
    pallas_call x1, Pallas kernels, body(): pl.pallas_call(functools.partial(outside_kernel, tile, SLICES), out_shape...  11.9 us
    ppermute x4, starting transfers between devices, body(): got = lax.ppermute(total, 'seq', [(i, i ^ step) for i in range(devices)])  8.27 us
    pallas_call x1, Pallas kernels, body(): pl.pallas_call(functools.partial(states_kernel, tile), out_shape=[split_s...  8.06 us
    ppermute x4, waiting for transfers between devices, body(): got = lax.ppermute(total, 'seq', [(i, i ^ step) for i in range(devices)])  3.44 us
  transfers between devices with their start and end apart: 6, of which 2 were waited for; matrix products, arithmetic and copies ran while one was open for 0% of the time, Pallas kernels for 35%

commit v1 on v0

v1 whole, which is shorter than its diff:
```python
import functools

import jax
import jax.numpy as jnp
from jax import lax
from jax.experimental import pallas as pl
from jax.experimental.pallas import tpu as pltpu
from jax.sharding import PartitionSpec as P

HEAD = 128
HEADS = 2
CHUNK = 128
CUTS = (3, 7, 7, 6, 6, 3)
SLICES = len(CUTS)

BF16 = jnp.bfloat16
F32 = jnp.float32
NAT = (((1,), (0,)), ((), ()))
ROWS = (((1,), (1,)), ((), ()))
COLS = (((0,), (0,)), ((), ()))
MIB = 1024 * 1024


def cut_sizes(chunks):
    edges = [sum(CUTS[:i]) * chunks // sum(CUTS) for i in range(SLICES + 1)]
    return [b - a for a, b in zip(edges, edges[1:])], edges[:-1]


def mm(a, b, dims=NAT):
    return lax.dot_general(a, b, dims, preferred_element_type=F32)


def parts(x):
    hi = x.astype(BF16)
    lo = (x - hi.astype(F32)).astype(BF16)
    return hi, lo


def pair(x):
    return jnp.concatenate(parts(x), axis=1)


def stacked(xx):
    hi, lo = xx[:, :HEAD], xx[:, HEAD:]
    top = jnp.concatenate([hi, hi], axis=1)
    low = jnp.concatenate([lo, lo], axis=1)
    return jnp.concatenate([top, low], axis=0)


def halves(x):
    return x[:, :HEAD] + x[:, HEAD:]


def twice(xx):
    return jnp.concatenate([xx, xx], axis=0)


def gram(hi, lo, yy):
    return halves(mm(jnp.concatenate([hi, lo], axis=0), twice(yy), COLS))


def states_kernel(tile, q, k, v, g, ks, vs, gs, mine, other, *rest):
    qs, pt, sg, sgt = (rest[j * SLICES : (j + 1) * SLICES] for j in range(4))
    kb, vb, qb, gb, own, sems = rest[4 * SLICES :]
    tokens = q.shape[0] // HEADS
    steps = tokens // tile
    rows = tile * HEADS
    per = tile // CHUNK
    place = [(i, n) for i, size in enumerate(cut_sizes(tokens // CHUNK)[0]) for n in range(size)]

    def fetch(step):
        back = steps - 1 - step
        return [
            pltpu.make_async_copy(src.at[pl.ds(at * rows, rows)], dst.at[step], sems.at[j, step])
            for j, (src, dst, at) in enumerate(((k, kb, step), (v, vb, step), (q, qb, back), (g, gb, back)))
        ]

    for step in range(steps):
        for c in fetch(step):
            c.start()
    core = lax.rem(lax.axis_index("seq"), 2)
    own[...] = jnp.zeros_like(own)
    for step in range(steps):
        for c in fetch(step):
            c.wait()
        back = steps - 1 - step
        for h in range(HEADS):
            p, s = own[0, h], own[1, h]
            for c in range(per):
                n = step * per + c
                tok = slice(n * CHUNK, (n + 1) * CHUNK)
                inside = pl.ds(c * CHUNK * HEADS + h, CHUNK, HEADS)
                kk = pair(kb[step, inside, :])
                vhi, vlo = parts(vb[step, inside, :])
                ks[h, tok, :] = kk
                vs[h, tok, :] = jnp.concatenate([vhi, vlo], axis=1)
                i, m = place[n]
                pt[i][m, h] = pair(p)
                p = p + gram(vhi, vlo, kk)

                r = per - 1 - c
                n = back * per + r
                tok = slice(n * CHUNK, (n + 1) * CHUNK)
                inside = pl.ds(r * CHUNK * HEADS + h, CHUNK, HEADS)
                qhi, qlo = parts(qb[step, inside, :])
                gg = pair(gb[step, inside, :])
                i, m = place[n]
                qs[i][h, m * CHUNK : (m + 1) * CHUNK, :] = jnp.concatenate([qhi, qlo], axis=1)
                gs[h, tok, :] = gg
                shi, slo = parts(s)
                sg[i][m, h] = jnp.concatenate([shi, slo], axis=1)
                sgt[i][m, h] = jnp.concatenate([shi.T, slo.T], axis=1)
                s = s + gram(qhi, qlo, gg)
            own[0, h] = p
            own[1, h] = s
    mine[...] = own[core]
    other[...] = own[1 - core]


def first_kernel(mine, got, order, total):
    total[...] = mine[...] + got[...]


def scan_kernel(step, first, last, mine, total, got, order, *rest):
    *entered, new_total, new_entered = rest
    here = lax.axis_index("seq")
    core = lax.rem(here, 2)
    bit = lax.rem(lax.div(here, step), 2)
    take = jnp.where(bit + core == 1, 1.0, 0.0)
    new = got[...] * take
    if not first:
        new += entered[0][...]
    new_entered[...] = new
    new_total[...] = new + mine[...] if last else total[...] + got[...]


def inside_kernel(first, count, qs, ks, vs, gs, pt, sg, sgt, order, dq, dk, dv):
    at_row = lax.broadcasted_iota(jnp.int32, (CHUNK, CHUNK), 0)
    at_col = lax.broadcasted_iota(jnp.int32, (CHUNK, CHUNK), 1)
    upper = at_row <= at_col
    lower = at_row >= at_col
    for n in range(count):
        for h in range(HEADS):
            tok = slice((first + n) * CHUNK, (first + n + 1) * CHUNK)
            out = slice(n * CHUNK, (n + 1) * CHUNK)
            kk, vv, gg = (x[h, tok, :] for x in (ks, vs, gs))
            qq = qs[h, out, :]

            def finish(score, keep, left, right, state):
                near = pair(jnp.where(keep, halves(score), 0.0))
                return halves(mm(near, twice(right)) + mm(left, twice(state)))

            dq[h, out, :] = finish(mm(gg, stacked(vv), ROWS), lower, gg, kk, pt[n, h])
            dk[h, out, :] = finish(mm(vv, stacked(gg), ROWS), upper, vv, qq, sgt[n, h])
            dv[h, out, :] = finish(mm(kk, stacked(qq), ROWS), upper, kk, gg, sg[n, h])


def outside_kernel(ks, vs, gs, entered, got, *rest):
    partial = rest[: 3 * SLICES]
    outs = rest[3 * SLICES : 3 * SLICES + 3]
    obs = rest[3 * SLICES + 3 : -1]
    sems = rest[-1]
    sizes, firsts = cut_sizes(ks.shape[1] // CHUNK)
    even = lax.rem(lax.axis_index("seq"), 2) == 0
    weights = []
    for h in range(HEADS):
        before = jnp.where(even, entered[h], got[h])
        after = jnp.where(even, got[h], entered[h])
        weights.append([twice(pair(w)) for w in (before, after.T, after)])

    def send(j, i):
        rows = pl.ds(firsts[i] * CHUNK * HEADS, sizes[i] * CHUNK * HEADS)
        return pltpu.make_async_copy(obs[i].at[j], outs[j].at[rows], sems.at[j, i])

    for j in range(3):
        for i in range(SLICES):
            tile = sizes[i] * CHUNK
            base = firsts[i] * CHUNK
            for h in range(HEADS):
                x = halves(mm((gs, vs, ks)[j][h, base : base + tile, :], weights[h][j]))
                obs[i][j, pl.ds(h, tile, HEADS), :] = x + partial[3 * i + j][h]
            send(j, i).start()
    for j in range(3):
        for i in range(SLICES):
            send(j, i).wait()


VM = pl.BlockSpec(memory_space=pltpu.VMEM)
ANY = pl.BlockSpec(memory_space=pl.ANY)


def vmem(*arrays):
    return [pltpu.with_memory_space_constraint(a, pltpu.VMEM) for a in arrays]


def hbm(*arrays):
    return [pltpu.with_memory_space_constraint(a, pltpu.HBM) for a in arrays]


def body(sizes, queries, key_vectors, value_vectors, grad_output):
    tokens = queries.shape[0]
    chunks = tokens // CHUNK
    flat = [x.reshape(tokens * HEADS, HEAD) for x in (queries, key_vectors, value_vectors, grad_output)]

    tile = 512
    split_shape = pltpu.VMEM((HEADS, tokens, 2 * HEAD), BF16)
    cuts, firsts = cut_sizes(chunks)
    query_shapes = [pltpu.VMEM((HEADS, n * CHUNK, 2 * HEAD), BF16) for n in cuts]
    state_shapes = [pltpu.VMEM((n, HEADS, HEAD, 2 * HEAD), BF16) for n in cuts]
    own_shape = pltpu.VMEM((HEADS, HEAD, HEAD), F32)
    shapes = [split_shape] * 3 + [own_shape] * 2 + query_shapes + state_shapes * 3
    ks, vs, gs, mine, other, *kept = pl.pallas_call(
        functools.partial(states_kernel, tile),
        out_shape=shapes,
        in_specs=[ANY] * 4,
        out_specs=[VM] * len(shapes),
        scratch_shapes=[pltpu.VMEM((tokens // tile, tile * HEADS, HEAD), F32)] * 4
        + [pltpu.VMEM((2, HEADS, HEAD, HEAD), F32), pltpu.SemaphoreType.DMA((4, tokens // tile))],
        compiler_params=pltpu.CompilerParams(vmem_limit_bytes=20 * MIB),
        cost_estimate=pl.CostEstimate(flops=10**9, bytes_accessed=16 * MIB, transcendentals=0),
        name="states",
    )(*hbm(*flat))

    def small(kernel, name, outs, *args):
        return pl.pallas_call(
            kernel,
            out_shape=[own_shape] * outs,
            in_specs=[VM] * len(args),
            out_specs=[VM] * outs,
            compiler_params=pltpu.CompilerParams(vmem_limit_bytes=2 * MIB),
            cost_estimate=pl.CostEstimate(flops=10**5, bytes_accessed=MIB, transcendentals=0),
            name=name,
        )(*vmem(*args))

    partial = []

    def inside(order):
        at = len(partial) // 3
        n = cuts[at]
        made = pl.pallas_call(
            functools.partial(inside_kernel, firsts[at], n),
            out_shape=[pltpu.VMEM((HEADS, n * CHUNK, HEAD), F32)] * 3,
            in_specs=[VM] * 8,
            out_specs=[VM] * 3,
            compiler_params=pltpu.CompilerParams(vmem_limit_bytes=4 * MIB),
            cost_estimate=pl.CostEstimate(flops=n * 4 * 10**8, bytes_accessed=MIB, transcendentals=0),
            name="inside" + str(at),
        )(*vmem(kept[at], ks, vs, gs, *kept[SLICES + at :: SLICES], order))
        partial.extend(made)
        return made[0]

    devices = sizes["seq"]
    sibling = [(i, i ^ 1) for i in range(devices)]
    got = lax.ppermute(other, "seq", sibling)
    (total,) = small(first_kernel, "first", 1, mine, got, inside(other))
    entered = []
    step = 2
    while step < devices:
        got = lax.ppermute(total, "seq", [(i, i ^ step) for i in range(devices)])
        kernel = functools.partial(scan_kernel, step, step == 2, step * 2 >= devices)
        total, *entered = small(kernel, "scan" + str(step), 2, mine, total, got, inside(total), *entered)
        step *= 2
    got = lax.ppermute(total, "seq", sibling)
    while len(partial) < 3 * SLICES:
        inside(total)

    out = pl.pallas_call(
        outside_kernel,
        out_shape=[pltpu.HBM((tokens * HEADS, HEAD), F32)] * 3,
        in_specs=[VM] * (5 + 3 * SLICES),
        out_specs=[ANY] * 3,
        scratch_shapes=[pltpu.VMEM((3, n * CHUNK * HEADS, HEAD), F32) for n in cuts]
        + [pltpu.SemaphoreType.DMA((3, SLICES))],
        compiler_params=pltpu.CompilerParams(vmem_limit_bytes=14 * MIB),
        cost_estimate=pl.CostEstimate(flops=10**9, bytes_accessed=12 * MIB, transcendentals=0),
        name="outside",
    )(*vmem(ks, vs, gs, *entered, got, *partial))
    return tuple(x.reshape(queries.shape) for x in out)


def solution(mesh):
    spec = P(("seqs", "seq"), None, None)
    return jax.shard_map(
        functools.partial(body, dict(mesh.shape)),
        mesh=mesh,
        in_specs=(spec,) * 4,
        out_specs=(spec,) * 3,
        check_vma=False,
    )
```

time: 119 us -> 43.3 us (0.36)
  local copies, waits for them, and re-layouts: 38.4 us -> 0 us
  Pallas kernels: 61.5 us -> 28.2 us
  waiting for transfers between devices: 4.43 us -> 0.58 us
  starting transfers between devices: 10.9 us -> 13.5 us
  other arithmetic: 1.87 us -> 0 us
    unnamed x76 -> x0, local copies, waits for them, and re-layouts: 38.4 us -> none
    pallas_call x6 -> x13, Pallas kernels: 61.5 us -> 28.2 us  [the longest x6 15.2 us: inside(): pl.pallas_call(functools.partial(inside_kernel, firsts[at], n), out_shape...]
    ppermute x4, waiting for transfers between devices: 3.44 us -> 0.58 us  [body(): got = lax.ppermute(total, 'seq', [(i, i ^ step) for i in range(devices)])]
    ppermute x2, starting transfers between devices: 2.58 us -> 4.94 us  [the longest x1 3.44 us: body(): got = lax.ppermute(total, 'seq', sibling)]
    add x5 -> x0, other arithmetic: 1.83 us -> none  [the longest x1 1.08 us: body(): got = lax.ppermute(entered + mine, 'seq', sibling)]
  transfers between devices with their start and end apart: 6 -> 6, of which waited for: 2 -> 1; matrix products, arithmetic and copies ran while one was open for 0% -> 0% of each run, Pallas kernels for 35% -> 35%
where the time goes in v1:
time: 43.3 us; the launch traced here: 43.1 us
  Pallas kernels  28.2 us (65%)
  starting transfers between devices  13.5 us (31%)
  between operations  0.95 us (2%)
  waiting for transfers between devices  0.58 us (1%)
    pallas_call x6, Pallas kernels, inside(): pl.pallas_call(functools.partial(inside_kernel, firsts[at], n), out_shape...  15.2 us
    ppermute x4, starting transfers between devices, body(): got = lax.ppermute(total, 'seq', [(i, i ^ step) for i in range(devices)])  8.52 us
    pallas_call x1, Pallas kernels, body(): pl.pallas_call(functools.partial(states_kernel, tile), out_shape=shapes,...  7.04 us
    pallas_call x1, Pallas kernels, body(): pl.pallas_call(outside_kernel, out_shape=[pltpu.HBM((tokens * HEADS, HEAD...  5.72 us
    ppermute x1, starting transfers between devices, body(): got = lax.ppermute(total, 'seq', sibling)  3.44 us
    ppermute x1, starting transfers between devices, body(): got = lax.ppermute(other, 'seq', sibling)  1.5 us
  transfers between devices with their start and end apart: 6, of which 1 were waited for; matrix products, arithmetic and copies ran while one was open for 0% of the time, Pallas kernels for 35%

profile of v1, /device:TPU:1, one launch (start us, length us, event | category | flops | bytes accessed | tf_op | source)
XLA Modules:
  0.0 43.1 jit_solution(12369069763529069097)
XLA Ops:
  0.6 7.0 %states.1 = (bf16[2,4096,256]{2,1,0:T(8,128)(2,1)S(1)}, bf16[2,4096,256]{2,1,0:T(8,128)(2,1)S(1)}, bf16[2,4096,256]{2,1,0:T(8,128)(2,1)S(1)}, f32[2,128,128]{2,1...) custom-call(f32[8192,128]{1,0:T(8,128)} %bitcast.7, ...), custom_call_target="tpu_custom_call" | custom-call | flops 1000000000 | bytes 16777216 | tf_op jit(solution)/shard_map/states/pallas_call | solution.py:212
  7.7 1.5 %collective-permute-start = (f32[2,128,128]{2,1,0:T(8,128)S(1)}, f32[2,128,128]{2,1,0:T(8,128)S(1)}, u32[]{:S(2)}, u32[]{:S(2)}) collective-permute-start(f32[2,128,128]{2,1,0:T(8,128)S(1)} %get-tuple-element.65.order), channel_id=1, source_target_pairs={{0,4},{4,0},{8,12},{12,8},{16,20},{20,16},{24,28},{28,24},{32,36},... | collective-permute-start | bytes 393224 | tf_op jit(solution)/shard_map/ppermute | solution.py:254
  9.2 1.5 %inside0.1 = (f32[2,384,128]{2,1,0:T(8,128)S(1)}, f32[2,384,128]{2,1,0:T(8,128)S(1)}, f32[2,384,128]{2,1,0:T(8,128)S(1)}) custom-call(bf16[2,384,256]{2,1,0:T(8,128)(2,1)S(1)} %get-tuple-element.66.qs, bf16[2,4096,256]{2,1,0:T(8,128)(2,1)S(1)} %get-tuple-element.61.ks, bf16[2,4096,256]{2,1,0:T(8,128)(2,1)S(1)} %get-tuple-element.62.vs, ...), custom_call_target="tpu_custom_call" | custom-call | flops 1200000000 | bytes 1048576 | tf_op jit(solution)/shard_map/inside0/pallas_call | solution.py:240
  10.7 0.0 collective-permute-done.got
  10.8 1.4 %collective-permute-start.1 = (f32[2,128,128]{2,1,0:T(8,128)S(1)}, f32[2,128,128]{2,1,0:T(8,128)S(1)}, u32[]{:S(2)}, u32[]{:S(2)}) collective-permute-start(f32[2,128,128]{2,1,0:T(8,128)S(1)} %first.1.order.total), channel_id=1, source_target_pairs={{0,8},{4,12},{8,0},{12,4},{16,24},{20,28},{24,16},{28,20},{32,40},... | collective-permute-start | bytes 393224 | tf_op jit(solution)/shard_map/ppermute | solution.py:259
  12.1 3.3 %inside1.1 = (f32[2,896,128]{2,1,0:T(8,128)S(1)}, f32[2,896,128]{2,1,0:T(8,128)S(1)}, f32[2,896,128]{2,1,0:T(8,128)S(1)}) custom-call(bf16[2,896,256]{2,1,0:T(8,128)(2,1)S(1)} %get-tuple-element.71.qs, bf16[2,4096,256]{2,1,0:T(8,128)(2,1)S(1)} %get-tuple-element.61.ks, bf16[2,4096,256]{2,1,0:T(8,128)(2,1)S(1)} %get-tuple-element.62.vs, ...), custom_call_target="tpu_custom_call" | custom-call | flops 2800000000 | bytes 1048576 | tf_op jit(solution)/shard_map/inside1/pallas_call | solution.py:240
  15.4 0.6 %collective-permute-done.1.got = f32[2,128,128]{2,1,0:T(8,128)S(1)} collective-permute-done((f32[2,128,128]{2,1,0:T(8,128)S(1)}, f32[2,128,128]{2,1,0:T(8,128)S(1)}, u32[]{:S(2)}, u32[]{:S(2)}) %collective-permute-start.1) | collective-permute-done | bytes 131104 | tf_op jit(solution)/shard_map/ppermute | solution.py:259
  16.0 3.1 %collective-permute-start.2 = (f32[2,128,128]{2,1,0:T(8,128)S(1)}, f32[2,128,128]{2,1,0:T(8,128)S(1)}, u32[]{:S(2)}, u32[]{:S(2)}) collective-permute-start(f32[2,128,128]{2,1,0:T(8,128)S(1)} %get-tuple-element.76.order.total), channel_id=1, source_target_pairs={{0,16},{4,20},{8,24},{12,28},{16,0},{20,4},{24,8},{28,12},{32,48},... | collective-permute-start | bytes 393224 | tf_op jit(solution)/shard_map/ppermute | solution.py:259
  19.1 3.2 %inside2.1 = (f32[2,896,128]{2,1,0:T(8,128)S(1)}, f32[2,896,128]{2,1,0:T(8,128)S(1)}, f32[2,896,128]{2,1,0:T(8,128)S(1)}) custom-call(bf16[2,896,256]{2,1,0:T(8,128)(2,1)S(1)} %get-tuple-element.77.qs, bf16[2,4096,256]{2,1,0:T(8,128)(2,1)S(1)} %get-tuple-element.61.ks, bf16[2,4096,256]{2,1,0:T(8,128)(2,1)S(1)} %get-tuple-element.62.vs, ...), custom_call_target="tpu_custom_call" | custom-call | flops 2800000000 | bytes 1048576 | tf_op jit(solution)/shard_map/inside2/pallas_call | solution.py:240
  22.3 0.0 collective-permute-done.2.got
  22.4 1.4 %collective-permute-start.3 = (f32[2,128,128]{2,1,0:T(8,128)S(1)}, f32[2,128,128]{2,1,0:T(8,128)S(1)}, u32[]{:S(2)}, u32[]{:S(2)}) collective-permute-start(f32[2,128,128]{2,1,0:T(8,128)S(1)} %get-tuple-element.83.order.total), channel_id=1, source_target_pairs={{0,32},{4,36},{8,40},{12,44},{16,48},{20,52},{24,56},{28,60},{32,0... | collective-permute-start | bytes 393224 | tf_op jit(solution)/shard_map/ppermute | solution.py:259
  23.8 2.8 %inside3.1 = (f32[2,768,128]{2,1,0:T(8,128)S(1)}, f32[2,768,128]{2,1,0:T(8,128)S(1)}, f32[2,768,128]{2,1,0:T(8,128)S(1)}) custom-call(bf16[2,768,256]{2,1,0:T(8,128)(2,1)S(1)} %get-tuple-element.84.qs, bf16[2,4096,256]{2,1,0:T(8,128)(2,1)S(1)} %get-tuple-element.61.ks, bf16[2,4096,256]{2,1,0:T(8,128)(2,1)S(1)} %get-tuple-element.62.vs, ...), custom_call_target="tpu_custom_call" | custom-call | flops 2400000000 | bytes 1048576 | tf_op jit(solution)/shard_map/inside3/pallas_call | solution.py:240
  26.6 0.0 collective-permute-done.3.got
  26.7 2.7 %collective-permute-start.4 = (f32[2,128,128]{2,1,0:T(8,128)S(1)}, f32[2,128,128]{2,1,0:T(8,128)S(1)}, u32[]{:S(2)}, u32[]{:S(2)}) collective-permute-start(f32[2,128,128]{2,1,0:T(8,128)S(1)} %get-tuple-element.90.order.total), channel_id=1, source_target_pairs={{0,64},{4,68},{8,72},{12,76},{16,80},{20,84},{24,88},{28,92},{32,9... | collective-permute-start | bytes 393224 | tf_op jit(solution)/shard_map/ppermute | solution.py:259
  29.3 2.8 %inside4.1 = (f32[2,768,128]{2,1,0:T(8,128)S(1)}, f32[2,768,128]{2,1,0:T(8,128)S(1)}, f32[2,768,128]{2,1,0:T(8,128)S(1)}) custom-call(bf16[2,768,256]{2,1,0:T(8,128)(2,1)S(1)} %get-tuple-element.91.qs, bf16[2,4096,256]{2,1,0:T(8,128)(2,1)S(1)} %get-tuple-element.61.ks, bf16[2,4096,256]{2,1,0:T(8,128)(2,1)S(1)} %get-tuple-element.62.vs, ...), custom_call_target="tpu_custom_call" | custom-call | flops 2400000000 | bytes 1048576 | tf_op jit(solution)/shard_map/inside4/pallas_call | solution.py:240
  32.2 0.0 collective-permute-done.4.got
  32.2 3.4 %collective-permute-start.5 = (f32[2,128,128]{2,1,0:T(8,128)S(1)}, f32[2,128,128]{2,1,0:T(8,128)S(1)}, u32[]{:S(2)}, u32[]{:S(2)}) collective-permute-start(f32[2,128,128]{2,1,0:T(8,128)S(1)} %get-tuple-element.98.order), channel_id=1, source_target_pairs={{0,4},{4,0},{8,12},{12,8},{16,20},{20,16},{24,28},{28,24},{32,36},... | collective-permute-start | bytes 393224 | tf_op jit(solution)/shard_map/ppermute | solution.py:263
  35.7 1.5 %inside5.1 = (f32[2,384,128]{2,1,0:T(8,128)S(1)}, f32[2,384,128]{2,1,0:T(8,128)S(1)}, f32[2,384,128]{2,1,0:T(8,128)S(1)}) custom-call(bf16[2,384,256]{2,1,0:T(8,128)(2,1)S(1)} %get-tuple-element.109.qs, bf16[2,4096,256]{2,1,0:T(8,128)(2,1)S(1)} %get-tuple-element.61.ks, bf16[2,4096,256]{2,1,0:T(8,128)(2,1)S(1)} %get-tuple-element.62.vs, ...), custom_call_target="tpu_custom_call" | custom-call | flops 1200000000 | bytes 1048576 | tf_op jit(solution)/shard_map/inside5/pallas_call | solution.py:240
  37.2 0.0 collective-permute-done.5.got
  37.2 5.7 %outside.1 = (f32[8192,128]{1,0:T(8,128)}, f32[8192,128]{1,0:T(8,128)}, f32[8192,128]{1,0:T(8,128)}) custom-call(bf16[2,4096,256]{2,1,0:T(8,128)(2,1)S(1)} %get-tuple-element.61.ks, bf16[2,4096,256]{2,1,0:T(8,128)(2,1)S(1)} %get-tuple-element.62.vs, bf16[2,4096,256]{2,1,0:T(8,128)(2,1)S(1)} %get-tuple-element.63.gs, ...), custom_call_target="tpu_custom_call" | custom-call | flops 1000000000 | bytes 12582912 | tf_op jit(solution)/shard_map/outside/pallas_call | solution.py:267
  (5 shorter events, 0.1 us)
Async XLA Ops:
  7.7 3.1 %collective-permute-start = (f32[2,128,128]{2,1,0:T(8,128)S(1)}, f32[2,128,128]{2,1,0:T(8,128)S(1)}, u32[]{:S(2)}, u32[]{:S(2)}) collective-permute-start(f32[2,128,128]{2,1,0:T(8,128)S(1)} %get-tuple-element.65.order), channel_id=1, source_target_pairs={{0,4},{4,0},{8,12},{12,8},{16,20},{20,16},{24,28},{28,24},{32,36},... | collective-permute-start | bytes 393224 | tf_op jit(solution)/shard_map/ppermute | solution.py:254
  10.8 5.2 %collective-permute-start.1 = (f32[2,128,128]{2,1,0:T(8,128)S(1)}, f32[2,128,128]{2,1,0:T(8,128)S(1)}, u32[]{:S(2)}, u32[]{:S(2)}) collective-permute-start(f32[2,128,128]{2,1,0:T(8,128)S(1)} %first.1.order.total), channel_id=1, source_target_pairs={{0,8},{4,12},{8,0},{12,4},{16,24},{20,28},{24,16},{28,20},{32,40},... | collective-permute-start | bytes 393224 | tf_op jit(solution)/shard_map/ppermute | solution.py:259
  16.0 6.3 %collective-permute-start.2 = (f32[2,128,128]{2,1,0:T(8,128)S(1)}, f32[2,128,128]{2,1,0:T(8,128)S(1)}, u32[]{:S(2)}, u32[]{:S(2)}) collective-permute-start(f32[2,128,128]{2,1,0:T(8,128)S(1)} %get-tuple-element.76.order.total), channel_id=1, source_target_pairs={{0,16},{4,20},{8,24},{12,28},{16,0},{20,4},{24,8},{28,12},{32,48},... | collective-permute-start | bytes 393224 | tf_op jit(solution)/shard_map/ppermute | solution.py:259
  22.4 4.2 %collective-permute-start.3 = (f32[2,128,128]{2,1,0:T(8,128)S(1)}, f32[2,128,128]{2,1,0:T(8,128)S(1)}, u32[]{:S(2)}, u32[]{:S(2)}) collective-permute-start(f32[2,128,128]{2,1,0:T(8,128)S(1)} %get-tuple-element.83.order.total), channel_id=1, source_target_pairs={{0,32},{4,36},{8,40},{12,44},{16,48},{20,52},{24,56},{28,60},{32,0... | collective-permute-start | bytes 393224 | tf_op jit(solution)/shard_map/ppermute | solution.py:259
  26.7 5.5 %collective-permute-start.4 = (f32[2,128,128]{2,1,0:T(8,128)S(1)}, f32[2,128,128]{2,1,0:T(8,128)S(1)}, u32[]{:S(2)}, u32[]{:S(2)}) collective-permute-start(f32[2,128,128]{2,1,0:T(8,128)S(1)} %get-tuple-element.90.order.total), channel_id=1, source_target_pairs={{0,64},{4,68},{8,72},{12,76},{16,80},{20,84},{24,88},{28,92},{32,9... | collective-permute-start | bytes 393224 | tf_op jit(solution)/shard_map/ppermute | solution.py:259
  32.2 5.0 %collective-permute-start.5 = (f32[2,128,128]{2,1,0:T(8,128)S(1)}, f32[2,128,128]{2,1,0:T(8,128)S(1)}, u32[]{:S(2)}, u32[]{:S(2)}) collective-permute-start(f32[2,128,128]{2,1,0:T(8,128)S(1)} %get-tuple-element.98.order), channel_id=1, source_target_pairs={{0,4},{4,0},{8,12},{12,8},{16,20},{20,16},{24,28},{28,24},{32,36},... | collective-permute-start | bytes 393224 | tf_op jit(solution)/shard_map/ppermute | solution.py:263

commit v2 on v1

--- a/solution.py
+++ b/solution.py
@@ -1,4 +1,5 @@
 import functools
+import math
 
 import jax
 import jax.numpy as jnp
@@ -10,7 +11,7 @@
 HEAD = 128
 HEADS = 2
 CHUNK = 128
-CUTS = (3, 7, 7, 6, 6, 3)
+CUTS = (3, 13, 13, 3)
 SLICES = len(CUTS)
 
 BF16 = jnp.bfloat16
@@ -117,21 +118,52 @@
     other[...] = own[1 - core]
 
 
-def first_kernel(mine, got, order, total):
-    total[...] = mine[...] + got[...]
-
-
-def scan_kernel(step, first, last, mine, total, got, order, *rest):
-    *entered, new_total, new_entered = rest
+def partners(here, low, high, second):
+    core = here % 2
+    step = low + (high - low) * (core + second - 2 * core * second)
+    return [here ^ (k * step) for k in range(1, 4)]
+
+
+def first_kernel(mine, got, order, chip):
+    chip[...] = mine[...] + got[...]
+
+
+def middle_kernel(low, high, chip, *rest):
+    *got, order, entered, m0, m1, m2 = rest
     here = lax.axis_index("seq")
-    core = lax.rem(here, 2)
-    bit = lax.rem(lax.div(here, step), 2)
-    take = jnp.where(bit + core == 1, 1.0, 0.0)
-    new = got[...] * take
-    if not first:
-        new += entered[0][...]
-    new_entered[...] = new
-    new_total[...] = new + mine[...] if last else total[...] + got[...]
+
+    def rows(low_first):
+        first = [here ^ (k * (low if low_first else high)) for k in range(1, 4)]
+        second = [here ^ (k * (high if low_first else low)) for k in range(1, 4)]
+        return first, second
+
+    @pl.when(lax.rem(here, 2) == 0)
+    def _():
+        first, _ = rows(True)
+        new = sum(g[...] * jnp.where(p < here, 1.0, 0.0) for g, p in zip(got, first))
+        entered[...] = new
+        total = chip[...] + got[0][...] + got[1][...] + got[2][...]
+        for m in (m0, m1, m2):
+            m[...] = total
+
+    @pl.when(lax.rem(here, 2) == 1)
+    def _():
+        first, second = rows(False)
+        new = sum(g[...] * jnp.where(p > here, 1.0, 0.0) for g, p in zip(got, first))
+        entered[...] = new
+        for m, p in zip((m0, m1, m2), second):
+            m[...] = new + chip[...] * jnp.where(p < here, 1.0, 0.0)
+
+
+def last_kernel(high, mine, before, *rest):
+    *got, order, entered, message = rest
+    here = lax.axis_index("seq")
+    new = before[...]
+    for k, g in enumerate(got):
+        use = (lax.rem(here, 2) == 1) | ((here ^ ((k + 1) * high)) < here)
+        new += g[...] * jnp.where(use, 1.0, 0.0)
+    entered[...] = new
+    message[...] = new + mine[...]
 
 
 def inside_kernel(first, count, qs, ks, vs, gs, pt, sg, sgt, order, dq, dk, dv):
@@ -252,17 +284,26 @@
     devices = sizes["seq"]
     sibling = [(i, i ^ 1) for i in range(devices)]
     got = lax.ppermute(other, "seq", sibling)
-    (total,) = small(first_kernel, "first", 1, mine, got, inside(other))
-    entered = []
-    step = 2
-    while step < devices:
-        got = lax.ppermute(total, "seq", [(i, i ^ step) for i in range(devices)])
-        kernel = functools.partial(scan_kernel, step, step == 2, step * 2 >= devices)
-        total, *entered = small(kernel, "scan" + str(step), 2, mine, total, got, inside(total), *entered)
-        step *= 2
-    got = lax.ppermute(total, "seq", sibling)
+    (chip,) = small(first_kernel, "first", 1, mine, got, inside(other))
+
+    side = math.isqrt(devices // 2)
+    low, high = 2, 2 * side
+
+    def swap(messages, second):
+        out = []
+        for k, m in enumerate(messages):
+            pairs = [(d, partners(d, low, high, second)[k]) for d in range(devices)]
+            out.append(lax.ppermute(m, "seq", pairs))
+        return out
+
+    got = swap([chip] * 3, 0)
+    entered, *messages = small(functools.partial(middle_kernel, low, high), "middle", 4, chip, *got, inside(chip))
+    got = swap(messages, 1)
+    kernel = functools.partial(last_kernel, high)
+    entered, message = small(kernel, "last", 2, mine, entered, *got, inside(messages[0]))
+    got = lax.ppermute(message, "seq", sibling)
     while len(partial) < 3 * SLICES:
-        inside(total)
+        inside(message)
 
     out = pl.pallas_call(
         outside_kernel,
@@ -274,7 +315,7 @@
         compiler_params=pltpu.CompilerParams(vmem_limit_bytes=14 * MIB),
         cost_estimate=pl.CostEstimate(flops=10**9, bytes_accessed=12 * MIB, transcendentals=0),
         name="outside",
-    )(*vmem(ks, vs, gs, *entered, got, *partial))
+    )(*vmem(ks, vs, gs, entered, got, *partial))
     return tuple(x.reshape(queries.shape) for x in out)
 
 

time: 43.3 us -> 38.7 us (0.89)
  starting transfers between devices: 13.5 us -> 10.2 us
  Pallas kernels: 28.2 us -> 27.4 us
  waiting for transfers between devices: 0.58 us -> 0.02 us
    ppermute x5 -> x7, starting transfers between devices: 12 us -> 8.69 us  [the longest x6 7.25 us: swap(): out.append(lax.ppermute(m, 'seq', pairs))]
    ppermute x5 -> x7, waiting for transfers between devices: 0.58 us -> 0.02 us  [the longest x6 0.02 us: swap(): out.append(lax.ppermute(m, 'seq', pairs))]
    pallas_call x6 -> x4, Pallas kernels: 15.2 us -> 14.7 us  [inside(): pl.pallas_call(functools.partial(inside_kernel, firsts[at], n), out_shape...]
  transfers between devices with their start and end apart: 6 -> 8, of which waited for: 1 -> 0; matrix products, arithmetic and copies ran while one was open for 0% -> 0% of each run, Pallas kernels for 35% -> 38%
where the time goes in v2:
time: 38.7 us; the launch traced here: 38.6 us
  Pallas kernels  27.4 us (71%)
  starting transfers between devices  10.2 us (26%)
  between operations  0.94 us (2%)
    pallas_call x4, Pallas kernels, inside(): pl.pallas_call(functools.partial(inside_kernel, firsts[at], n), out_shape...  14.7 us
    ppermute x6, starting transfers between devices, swap(): out.append(lax.ppermute(m, 'seq', pairs))  7.25 us
    pallas_call x1, Pallas kernels, body(): pl.pallas_call(functools.partial(states_kernel, tile), out_shape=shapes,...  7.03 us
    pallas_call x1, Pallas kernels, body(): pl.pallas_call(outside_kernel, out_shape=[pltpu.HBM((tokens * HEADS, HEAD...  5.52 us
    ppermute x1, starting transfers between devices, body(): got = lax.ppermute(other, 'seq', sibling)  1.5 us
    ppermute x1, starting transfers between devices, body(): got = lax.ppermute(message, 'seq', sibling)  1.43 us
  transfers between devices with their start and end apart: 8, of which 0 were waited for; matrix products, arithmetic and copies ran while one was open for 0% of the time, Pallas kernels for 38%

profile of v2, /device:TPU:1, one launch (start us, length us, event | category | flops | bytes accessed | tf_op | source)
XLA Modules:
  0.0 38.6 jit_solution(18023299840774772957)
XLA Ops:
  0.6 7.0 %states.1 = (bf16[2,4096,256]{2,1,0:T(8,128)(2,1)S(1)}, bf16[2,4096,256]{2,1,0:T(8,128)(2,1)S(1)}, bf16[2,4096,256]{2,1,0:T(8,128)(2,1)S(1)}, f32[2,128,128]{2,1...) custom-call(f32[8192,128]{1,0:T(8,128)} %bitcast.7, ...), custom_call_target="tpu_custom_call" | custom-call | flops 1000000000 | bytes 16777216 | tf_op jit(solution)/shard_map/states/pallas_call | solution.py:244
  7.7 1.5 %collective-permute-start = (f32[2,128,128]{2,1,0:T(8,128)S(1)}, f32[2,128,128]{2,1,0:T(8,128)S(1)}, u32[]{:S(2)}, u32[]{:S(2)}) collective-permute-start(f32[2,128,128]{2,1,0:T(8,128)S(1)} %get-tuple-element.49.order), channel_id=1, source_target_pairs={{0,4},{4,0},{8,12},{12,8},{16,20},{20,16},{24,28},{28,24},{32,36},... | collective-permute-start | bytes 393224 | tf_op jit(solution)/shard_map/ppermute | solution.py:286
  9.2 1.5 %inside0.1 = (f32[2,384,128]{2,1,0:T(8,128)S(1)}, f32[2,384,128]{2,1,0:T(8,128)S(1)}, f32[2,384,128]{2,1,0:T(8,128)S(1)}) custom-call(bf16[2,384,256]{2,1,0:T(8,128)(2,1)S(1)} %get-tuple-element.50.qs, bf16[2,4096,256]{2,1,0:T(8,128)(2,1)S(1)} %get-tuple-element.45.ks, bf16[2,4096,256]{2,1,0:T(8,128)(2,1)S(1)} %get-tuple-element.46.vs, ...), custom_call_target="tpu_custom_call" | custom-call | flops 1200000000 | bytes 1048576 | tf_op jit(solution)/shard_map/inside0/pallas_call | solution.py:272
  10.7 0.0 collective-permute-done.got
  10.8 2.9 %collective-permute-start.3 = (f32[2,128,128]{2,1,0:T(8,128)S(1)}, f32[2,128,128]{2,1,0:T(8,128)S(1)}, u32[]{:S(2)}, u32[]{:S(2)}) collective-permute-start(f32[2,128,128]{2,1,0:T(8,128)S(1)} %first.1.order.chip), channel_id=1, source_target_pairs={{0,24},{4,100},{8,16},{12,108},{16,8},{20,116},{24,0},{28,124},{32... | collective-permute-start | bytes 393224 | tf_op jit(solution)/shard_map/ppermute | solution.py:296
  13.6 0.4 collective-permute-start.2
  14.0 0.3 collective-permute-start.1
  14.3 5.8 %inside1.1 = (f32[2,1664,128]{2,1,0:T(8,128)S(1)}, f32[2,1664,128]{2,1,0:T(8,128)S(1)}, f32[2,1664,128]{2,1,0:T(8,128)S(1)}) custom-call(bf16[2,1664,256]{2,1,0:T(8,128)(2,1)S(1)} %get-tuple-element.55.qs, bf16[2,4096,256]{2,1,0:T(8,128)(2,1)S(1)} %get-tuple-element.45.ks, bf16[2,4096,256]{2,1,0:T(8,128)(2,1)S(1)} %get-tuple-element.46.vs, ...), custom_call_target="tpu_custom_call" | custom-call | flops 5200000000 | bytes 1048576 | tf_op jit(solution)/shard_map/inside1/pallas_call | solution.py:272
  20.1 0.0 collective-permute-done.3.rest_2_
  20.1 0.0 collective-permute-done.2.rest_1_
  20.2 0.0 collective-permute-done.1.rest_0_
  20.2 0.1 middle.1
  20.3 2.8 %collective-permute-start.5 = (f32[2,128,128]{2,1,0:T(8,128)S(1)}, f32[2,128,128]{2,1,0:T(8,128)S(1)}, u32[]{:S(2)}, u32[]{:S(2)}) collective-permute-start(f32[2,128,128]{2,1,0:T(8,128)S(1)} %get-tuple-element.62), channel_id=1, source_target_pairs={{0,64},{4,20},{8,72},{12,28},{16,80},{20,4},{24,88},{28,12},{32,96... | collective-permute-start | bytes 393224 | tf_op jit(solution)/shard_map/ppermute | solution.py:296
  23.1 0.9 %collective-permute-start.6 = (f32[2,128,128]{2,1,0:T(8,128)S(1)}, f32[2,128,128]{2,1,0:T(8,128)S(1)}, u32[]{:S(2)}, u32[]{:S(2)}) collective-permute-start(f32[2,128,128]{2,1,0:T(8,128)S(1)} %get-tuple-element.63), channel_id=1, source_target_pairs={{0,96},{4,28},{8,104},{12,20},{16,112},{20,12},{24,120},{28,4},{32... | collective-permute-start | bytes 393224 | tf_op jit(solution)/shard_map/ppermute | solution.py:296
  23.9 0.0 collective-permute-start.4
  23.9 5.8 %inside2.1 = (f32[2,1664,128]{2,1,0:T(8,128)S(1)}, f32[2,1664,128]{2,1,0:T(8,128)S(1)}, f32[2,1664,128]{2,1,0:T(8,128)S(1)}) custom-call(bf16[2,1664,256]{2,1,0:T(8,128)(2,1)S(1)} %get-tuple-element.64.qs, bf16[2,4096,256]{2,1,0:T(8,128)(2,1)S(1)} %get-tuple-element.45.ks, bf16[2,4096,256]{2,1,0:T(8,128)(2,1)S(1)} %get-tuple-element.46.vs, ...), custom_call_target="tpu_custom_call" | custom-call | flops 5200000000 | bytes 1048576 | tf_op jit(solution)/shard_map/inside2/pallas_call | solution.py:272
  29.8 0.0 collective-permute-done.5.rest_1_
  29.8 0.0 collective-permute-done.6.rest_2_
  29.8 0.0 collective-permute-done.4.rest_0_
  29.8 0.1 last.1
  29.9 1.4 %collective-permute-start.7 = (f32[2,128,128]{2,1,0:T(8,128)S(1)}, f32[2,128,128]{2,1,0:T(8,128)S(1)}, u32[]{:S(2)}, u32[]{:S(2)}) collective-permute-start(f32[2,128,128]{2,1,0:T(8,128)S(1)} %get-tuple-element.70.order), channel_id=1, source_target_pairs={{0,4},{4,0},{8,12},{12,8},{16,20},{20,16},{24,28},{28,24},{32,36},... | collective-permute-start | bytes 393224 | tf_op jit(solution)/shard_map/ppermute | solution.py:304
  31.3 1.5 %inside3.1 = (f32[2,384,128]{2,1,0:T(8,128)S(1)}, f32[2,384,128]{2,1,0:T(8,128)S(1)}, f32[2,384,128]{2,1,0:T(8,128)S(1)}) custom-call(bf16[2,384,256]{2,1,0:T(8,128)(2,1)S(1)} %get-tuple-element.77.qs, bf16[2,4096,256]{2,1,0:T(8,128)(2,1)S(1)} %get-tuple-element.45.ks, bf16[2,4096,256]{2,1,0:T(8,128)(2,1)S(1)} %get-tuple-element.46.vs, ...), custom_call_target="tpu_custom_call" | custom-call | flops 1200000000 | bytes 1048576 | tf_op jit(solution)/shard_map/inside3/pallas_call | solution.py:272
  32.8 0.0 collective-permute-done.7.got
  32.8 5.5 %outside.1 = (f32[8192,128]{1,0:T(8,128)}, f32[8192,128]{1,0:T(8,128)}, f32[8192,128]{1,0:T(8,128)}) custom-call(bf16[2,4096,256]{2,1,0:T(8,128)(2,1)S(1)} %get-tuple-element.45.ks, bf16[2,4096,256]{2,1,0:T(8,128)(2,1)S(1)} %get-tuple-element.46.vs, bf16[2,4096,256]{2,1,0:T(8,128)(2,1)S(1)} %get-tuple-element.47.gs, ...), custom_call_target="tpu_custom_call" | custom-call | flops 1000000000 | bytes 12582912 | tf_op jit(solution)/shard_map/outside/pallas_call | solution.py:308
  (1 shorter events, 0.0 us)
Async XLA Ops:
  7.7 3.1 %collective-permute-start = (f32[2,128,128]{2,1,0:T(8,128)S(1)}, f32[2,128,128]{2,1,0:T(8,128)S(1)}, u32[]{:S(2)}, u32[]{:S(2)}) collective-permute-start(f32[2,128,128]{2,1,0:T(8,128)S(1)} %get-tuple-element.49.order), channel_id=1, source_target_pairs={{0,4},{4,0},{8,12},{12,8},{16,20},{20,16},{24,28},{28,24},{32,36},... | collective-permute-start | bytes 393224 | tf_op jit(solution)/shard_map/ppermute | solution.py:286
  10.8 9.4 %collective-permute-start.3 = (f32[2,128,128]{2,1,0:T(8,128)S(1)}, f32[2,128,128]{2,1,0:T(8,128)S(1)}, u32[]{:S(2)}, u32[]{:S(2)}) collective-permute-start(f32[2,128,128]{2,1,0:T(8,128)S(1)} %first.1.order.chip), channel_id=1, source_target_pairs={{0,24},{4,100},{8,16},{12,108},{16,8},{20,116},{24,0},{28,124},{32... | collective-permute-start | bytes 393224 | tf_op jit(solution)/shard_map/ppermute | solution.py:296
  13.6 6.5 %collective-permute-start.2 = (f32[2,128,128]{2,1,0:T(8,128)S(1)}, f32[2,128,128]{2,1,0:T(8,128)S(1)}, u32[]{:S(2)}, u32[]{:S(2)}) collective-permute-start(f32[2,128,128]{2,1,0:T(8,128)S(1)} %first.1.order.chip), channel_id=1, source_target_pairs={{0,16},{4,68},{8,24},{12,76},{16,0},{20,84},{24,8},{28,92},{32,48}... | collective-permute-start | bytes 393224 | tf_op jit(solution)/shard_map/ppermute | solution.py:296
  14.0 6.2 %collective-permute-start.1 = (f32[2,128,128]{2,1,0:T(8,128)S(1)}, f32[2,128,128]{2,1,0:T(8,128)S(1)}, u32[]{:S(2)}, u32[]{:S(2)}) collective-permute-start(f32[2,128,128]{2,1,0:T(8,128)S(1)} %first.1.order.chip), channel_id=1, source_target_pairs={{0,8},{4,36},{8,0},{12,44},{16,24},{20,52},{24,16},{28,60},{32,40}... | collective-permute-start | bytes 393224 | tf_op jit(solution)/shard_map/ppermute | solution.py:296
  20.3 9.5 %collective-permute-start.5 = (f32[2,128,128]{2,1,0:T(8,128)S(1)}, f32[2,128,128]{2,1,0:T(8,128)S(1)}, u32[]{:S(2)}, u32[]{:S(2)}) collective-permute-start(f32[2,128,128]{2,1,0:T(8,128)S(1)} %get-tuple-element.62), channel_id=1, source_target_pairs={{0,64},{4,20},{8,72},{12,28},{16,80},{20,4},{24,88},{28,12},{32,96... | collective-permute-start | bytes 393224 | tf_op jit(solution)/shard_map/ppermute | solution.py:296
  23.1 6.7 %collective-permute-start.6 = (f32[2,128,128]{2,1,0:T(8,128)S(1)}, f32[2,128,128]{2,1,0:T(8,128)S(1)}, u32[]{:S(2)}, u32[]{:S(2)}) collective-permute-start(f32[2,128,128]{2,1,0:T(8,128)S(1)} %get-tuple-element.63), channel_id=1, source_target_pairs={{0,96},{4,28},{8,104},{12,20},{16,112},{20,12},{24,120},{28,4},{32... | collective-permute-start | bytes 393224 | tf_op jit(solution)/shard_map/ppermute | solution.py:296
  23.9 5.8 %collective-permute-start.4 = (f32[2,128,128]{2,1,0:T(8,128)S(1)}, f32[2,128,128]{2,1,0:T(8,128)S(1)}, u32[]{:S(2)}, u32[]{:S(2)}) collective-permute-start(f32[2,128,128]{2,1,0:T(8,128)S(1)} %get-tuple-element.61.order), channel_id=1, source_target_pairs={{0,32},{4,12},{8,40},{12,4},{16,48},{20,28},{24,56},{28,20},{32,0}... | collective-permute-start | bytes 393224 | tf_op jit(solution)/shard_map/ppermute | solution.py:296
  29.9 3.0 %collective-permute-start.7 = (f32[2,128,128]{2,1,0:T(8,128)S(1)}, f32[2,128,128]{2,1,0:T(8,128)S(1)}, u32[]{:S(2)}, u32[]{:S(2)}) collective-permute-start(f32[2,128,128]{2,1,0:T(8,128)S(1)} %get-tuple-element.70.order), channel_id=1, source_target_pairs={{0,4},{4,0},{8,12},{12,8},{16,20},{20,16},{24,28},{28,24},{32,36},... | collective-permute-start | bytes 393224 | tf_op jit(solution)/shard_map/ppermute | solution.py:304

commit v3 on v2

--- a/solution.py
+++ b/solution.py
@@ -12,6 +12,8 @@
 HEADS = 2
 CHUNK = 128
 CUTS = (3, 13, 13, 3)
+LEAD = 4
+PIECE = 5
 SLICES = len(CUTS)
 
 BF16 = jnp.bfloat16
@@ -25,6 +27,15 @@
 def cut_sizes(chunks):
     edges = [sum(CUTS[:i]) * chunks // sum(CUTS) for i in range(SLICES + 1)]
     return [b - a for a, b in zip(edges, edges[1:])], edges[:-1]
+
+
+def piece_list(sizes):
+    pieces = []
+    for i, size in enumerate(sizes):
+        count = -(-size // PIECE)
+        edges = [size * n // count for n in range(count + 1)]
+        pieces += [(i, a, b - a) for a, b in zip(edges, edges[1:])]
+    return pieces
 
 
 def mm(a, b, dims=NAT):
@@ -124,8 +135,10 @@
     return [here ^ (k * step) for k in range(1, 4)]
 
 
-def first_kernel(mine, got, order, chip):
-    chip[...] = mine[...] + got[...]
+def first_kernel(mine, got, order, *chip):
+    new = mine[...] + got[...]
+    for c in chip:
+        c[...] = new
 
 
 def middle_kernel(low, high, chip, *rest):
@@ -171,20 +184,36 @@
     at_col = lax.broadcasted_iota(jnp.int32, (CHUNK, CHUNK), 1)
     upper = at_row <= at_col
     lower = at_row >= at_col
-    for n in range(count):
-        for h in range(HEADS):
-            tok = slice((first + n) * CHUNK, (first + n + 1) * CHUNK)
-            out = slice(n * CHUNK, (n + 1) * CHUNK)
-            kk, vv, gg = (x[h, tok, :] for x in (ks, vs, gs))
-            qq = qs[h, out, :]
-
-            def finish(score, keep, left, right, state):
-                near = pair(jnp.where(keep, halves(score), 0.0))
-                return halves(mm(near, twice(right)) + mm(left, twice(state)))
-
-            dq[h, out, :] = finish(mm(gg, stacked(vv), ROWS), lower, gg, kk, pt[n, h])
-            dk[h, out, :] = finish(mm(vv, stacked(gg), ROWS), upper, vv, qq, sgt[n, h])
-            dv[h, out, :] = finish(mm(kk, stacked(qq), ROWS), upper, kk, gg, sg[n, h])
+    work = [(n, h, which) for n in range(count) for h in range(HEADS) for which in range(3)]
+
+    def load(n, h):
+        tok = slice((first + n) * CHUNK, (first + n + 1) * CHUNK)
+        return qs[h, n * CHUNK : (n + 1) * CHUNK, :], ks[h, tok, :], vs[h, tok, :], gs[h, tok, :]
+
+    def score(n, h, which):
+        qq, kk, vv, gg = load(n, h)
+        a, b = ((gg, vv), (vv, gg), (kk, qq))[which]
+        return halves(mm(a, stacked(b), ROWS))
+
+    def finish(near, n, h, which):
+        qq, kk, vv, gg = load(n, h)
+        keep, left, right, state, out = (
+            (lower, gg, kk, pt, dq),
+            (upper, vv, qq, sgt, dk),
+            (upper, kk, gg, sg, dv),
+        )[which]
+        hi, lo = parts(jnp.where(keep, near, 0.0))
+        top = jnp.concatenate([hi, left[:, :HEAD]], axis=1)
+        low = jnp.concatenate([lo, left[:, HEAD:]], axis=1)
+        x = mm(jnp.concatenate([top, low], axis=0), jnp.concatenate([right, state[n, h]], axis=0))
+        out[h, n * CHUNK : (n + 1) * CHUNK, :] = halves(x[:CHUNK]) + x[CHUNK:, :HEAD]
+
+    ready = []
+    for i in range(len(work) + LEAD):
+        if i < len(work):
+            ready.append(score(*work[i]))
+        if i >= LEAD:
+            finish(ready.pop(0), *work[i - LEAD])
 
 
 def outside_kernel(ks, vs, gs, entered, got, *rest):
@@ -193,6 +222,7 @@
     obs = rest[3 * SLICES + 3 : -1]
     sems = rest[-1]
     sizes, firsts = cut_sizes(ks.shape[1] // CHUNK)
+    pieces = piece_list(sizes)
     even = lax.rem(lax.axis_index("seq"), 2) == 0
     weights = []
     for h in range(HEADS):
@@ -200,21 +230,24 @@
         after = jnp.where(even, got[h], entered[h])
         weights.append([twice(pair(w)) for w in (before, after.T, after)])
 
-    def send(j, i):
-        rows = pl.ds(firsts[i] * CHUNK * HEADS, sizes[i] * CHUNK * HEADS)
-        return pltpu.make_async_copy(obs[i].at[j], outs[j].at[rows], sems.at[j, i])
-
-    for j in range(3):
-        for i in range(SLICES):
-            tile = sizes[i] * CHUNK
-            base = firsts[i] * CHUNK
-            for h in range(HEADS):
-                x = halves(mm((gs, vs, ks)[j][h, base : base + tile, :], weights[h][j]))
-                obs[i][j, pl.ds(h, tile, HEADS), :] = x + partial[3 * i + j][h]
-            send(j, i).start()
-    for j in range(3):
-        for i in range(SLICES):
-            send(j, i).wait()
+    def send(j, n):
+        i, first, size = pieces[n]
+        src = obs[i].at[j, pl.ds(first * CHUNK * HEADS, size * CHUNK * HEADS)]
+        dst = outs[j].at[pl.ds((firsts[i] + first) * CHUNK * HEADS, size * CHUNK * HEADS)]
+        return pltpu.make_async_copy(src, dst, sems.at[j, n])
+
+    work = [(j, n) for j in range(3) for n in range(len(pieces))]
+    for j, n in work:
+        i, first, size = pieces[n]
+        tile = size * CHUNK
+        off = first * CHUNK
+        base = firsts[i] * CHUNK + off
+        for h in range(HEADS):
+            x = halves(mm((gs, vs, ks)[j][h, base : base + tile, :], weights[h][j]))
+            obs[i][j, pl.ds(off * HEADS + h, tile, HEADS), :] = x + partial[3 * i + j][h, off : off + tile, :]
+        send(j, n).start()
+    for j, n in work:
+        send(j, n).wait()
 
 
 VM = pl.BlockSpec(memory_space=pltpu.VMEM)
@@ -284,7 +317,7 @@
     devices = sizes["seq"]
     sibling = [(i, i ^ 1) for i in range(devices)]
     got = lax.ppermute(other, "seq", sibling)
-    (chip,) = small(first_kernel, "first", 1, mine, got, inside(other))
+    chips = small(first_kernel, "first", 3, mine, got, inside(other))
 
     side = math.isqrt(devices // 2)
     low, high = 2, 2 * side
@@ -296,8 +329,8 @@
             out.append(lax.ppermute(m, "seq", pairs))
         return out
 
-    got = swap([chip] * 3, 0)
-    entered, *messages = small(functools.partial(middle_kernel, low, high), "middle", 4, chip, *got, inside(chip))
+    got = swap(chips, 0)
+    entered, *messages = small(functools.partial(middle_kernel, low, high), "middle", 4, chips[0], *got, inside(chips[0]))
     got = swap(messages, 1)
     kernel = functools.partial(last_kernel, high)
     entered, message = small(kernel, "last", 2, mine, entered, *got, inside(messages[0]))
@@ -311,7 +344,7 @@
         in_specs=[VM] * (5 + 3 * SLICES),
         out_specs=[ANY] * 3,
         scratch_shapes=[pltpu.VMEM((3, n * CHUNK * HEADS, HEAD), F32) for n in cuts]
-        + [pltpu.SemaphoreType.DMA((3, SLICES))],
+        + [pltpu.SemaphoreType.DMA((3, len(piece_list(cuts))))],
         compiler_params=pltpu.CompilerParams(vmem_limit_bytes=14 * MIB),
         cost_estimate=pl.CostEstimate(flops=10**9, bytes_accessed=12 * MIB, transcendentals=0),
         name="outside",

time: 38.7 us -> 36.4 us (0.941)
  Pallas kernels: 27.4 us -> 23.5 us
  starting transfers between devices: 10.2 us -> 11.7 us
    pallas_call x4, Pallas kernels: 14.7 us -> 11.3 us  [inside(): pl.pallas_call(functools.partial(inside_kernel, firsts[at], n), out_shape...]
    ppermute x1, starting transfers between devices: 1.43 us -> 2.78 us  [body(): got = lax.ppermute(message, 'seq', sibling)]
    pallas_call x1, Pallas kernels: 5.52 us -> 5.04 us  [body(): pl.pallas_call(outside_kernel, out_shape=[pltpu.HBM((tokens * HEADS, HEAD...]
  transfers between devices with their start and end apart: 8 -> 8, of which waited for: 0 -> 1; matrix products, arithmetic and copies ran while one was open for 0% -> 0% of each run, Pallas kernels for 38% -> 31%
where the time goes in v3:
time: 36.4 us; the launch traced here: 36.3 us
  Pallas kernels  23.5 us (65%)
  starting transfers between devices  11.7 us (32%)
  between operations  0.9 us (2%)
    pallas_call x4, Pallas kernels, inside(): pl.pallas_call(functools.partial(inside_kernel, firsts[at], n), out_shape...  11.3 us
    ppermute x6, starting transfers between devices, swap(): out.append(lax.ppermute(m, 'seq', pairs))  7.46 us
    pallas_call x1, Pallas kernels, body(): pl.pallas_call(functools.partial(states_kernel, tile), out_shape=shapes,...  7.03 us
    pallas_call x1, Pallas kernels, body(): pl.pallas_call(outside_kernel, out_shape=[pltpu.HBM((tokens * HEADS, HEAD...  5.04 us
    ppermute x1, starting transfers between devices, body(): got = lax.ppermute(message, 'seq', sibling)  2.78 us
    ppermute x1, starting transfers between devices, body(): got = lax.ppermute(other, 'seq', sibling)  1.5 us
  transfers between devices with their start and end apart: 8, of which 1 were waited for; matrix products, arithmetic and copies ran while one was open for 0% of the time, Pallas kernels for 31%

profile of v3, /device:TPU:1, one launch (start us, length us, event | category | flops | bytes accessed | tf_op | source)
XLA Modules:
  0.0 36.3 jit_solution(13860296446206348779)
XLA Ops:
  0.6 7.0 %states.1 = (bf16[2,4096,256]{2,1,0:T(8,128)(2,1)S(1)}, bf16[2,4096,256]{2,1,0:T(8,128)(2,1)S(1)}, bf16[2,4096,256]{2,1,0:T(8,128)(2,1)S(1)}, f32[2,128,128]{2,1...) custom-call(f32[8192,128]{1,0:T(8,128)} %bitcast.7, ...), custom_call_target="tpu_custom_call" | custom-call | flops 1000000000 | bytes 16777216 | tf_op jit(solution)/shard_map/states/pallas_call | solution.py:277
  7.7 1.5 %collective-permute-start = (f32[2,128,128]{2,1,0:T(8,128)S(1)}, f32[2,128,128]{2,1,0:T(8,128)S(1)}, u32[]{:S(2)}, u32[]{:S(2)}) collective-permute-start(f32[2,128,128]{2,1,0:T(8,128)S(1)} %get-tuple-element.52.order), channel_id=1, source_target_pairs={{0,4},{4,0},{8,12},{12,8},{16,20},{20,16},{24,28},{28,24},{32,36},... | collective-permute-start | bytes 393224 | tf_op jit(solution)/shard_map/ppermute | solution.py:319
  9.2 1.2 %inside0.1 = (f32[2,384,128]{2,1,0:T(8,128)S(1)}, f32[2,384,128]{2,1,0:T(8,128)S(1)}, f32[2,384,128]{2,1,0:T(8,128)S(1)}) custom-call(bf16[2,384,256]{2,1,0:T(8,128)(2,1)S(1)} %get-tuple-element.53.qs, bf16[2,4096,256]{2,1,0:T(8,128)(2,1)S(1)} %get-tuple-element.48.ks, bf16[2,4096,256]{2,1,0:T(8,128)(2,1)S(1)} %get-tuple-element.49.vs, ...), custom_call_target="tpu_custom_call" | custom-call | flops 1200000000 | bytes 1048576 | tf_op jit(solution)/shard_map/inside0/pallas_call | solution.py:305
  10.4 0.0 collective-permute-done.got
  10.4 3.1 %collective-permute-start.2 = (f32[2,128,128]{2,1,0:T(8,128)S(1)}, f32[2,128,128]{2,1,0:T(8,128)S(1)}, u32[]{:S(2)}, u32[]{:S(2)}) collective-permute-start(f32[2,128,128]{2,1,0:T(8,128)S(1)} %get-tuple-element.59), channel_id=1, source_target_pairs={{0,16},{4,68},{8,24},{12,76},{16,0},{20,84},{24,8},{28,92},{32,48}... | collective-permute-start | bytes 393224 | tf_op jit(solution)/shard_map/ppermute | solution.py:329
  13.5 0.8 %collective-permute-start.3 = (f32[2,128,128]{2,1,0:T(8,128)S(1)}, f32[2,128,128]{2,1,0:T(8,128)S(1)}, u32[]{:S(2)}, u32[]{:S(2)}) collective-permute-start(f32[2,128,128]{2,1,0:T(8,128)S(1)} %get-tuple-element.60), channel_id=1, source_target_pairs={{0,24},{4,100},{8,16},{12,108},{16,8},{20,116},{24,0},{28,124},{32... | collective-permute-start | bytes 393224 | tf_op jit(solution)/shard_map/ppermute | solution.py:329
  14.3 0.0 collective-permute-start.1
  14.3 4.4 %inside1.1 = (f32[2,1664,128]{2,1,0:T(8,128)S(1)}, f32[2,1664,128]{2,1,0:T(8,128)S(1)}, f32[2,1664,128]{2,1,0:T(8,128)S(1)}) custom-call(bf16[2,1664,256]{2,1,0:T(8,128)(2,1)S(1)} %get-tuple-element.61.qs, bf16[2,4096,256]{2,1,0:T(8,128)(2,1)S(1)} %get-tuple-element.48.ks, bf16[2,4096,256]{2,1,0:T(8,128)(2,1)S(1)} %get-tuple-element.49.vs, ...), custom_call_target="tpu_custom_call" | custom-call | flops 5200000000 | bytes 1048576 | tf_op jit(solution)/shard_map/inside1/pallas_call | solution.py:305
  18.7 0.0 collective-permute-done.2.rest_1_
  18.7 0.1 collective-permute-done.3.rest_2_
  18.8 0.0 collective-permute-done.1.rest_0_
  18.9 0.1 middle.1
  18.9 2.7 %collective-permute-start.5 = (f32[2,128,128]{2,1,0:T(8,128)S(1)}, f32[2,128,128]{2,1,0:T(8,128)S(1)}, u32[]{:S(2)}, u32[]{:S(2)}) collective-permute-start(f32[2,128,128]{2,1,0:T(8,128)S(1)} %get-tuple-element.68), channel_id=1, source_target_pairs={{0,64},{4,20},{8,72},{12,28},{16,80},{20,4},{24,88},{28,12},{32,96... | collective-permute-start | bytes 393224 | tf_op jit(solution)/shard_map/ppermute | solution.py:329
  21.7 0.9 %collective-permute-start.6 = (f32[2,128,128]{2,1,0:T(8,128)S(1)}, f32[2,128,128]{2,1,0:T(8,128)S(1)}, u32[]{:S(2)}, u32[]{:S(2)}) collective-permute-start(f32[2,128,128]{2,1,0:T(8,128)S(1)} %get-tuple-element.69), channel_id=1, source_target_pairs={{0,96},{4,28},{8,104},{12,20},{16,112},{20,12},{24,120},{28,4},{32... | collective-permute-start | bytes 393224 | tf_op jit(solution)/shard_map/ppermute | solution.py:329
  22.5 0.0 collective-permute-start.4
  22.5 4.4 %inside2.1 = (f32[2,1664,128]{2,1,0:T(8,128)S(1)}, f32[2,1664,128]{2,1,0:T(8,128)S(1)}, f32[2,1664,128]{2,1,0:T(8,128)S(1)}) custom-call(bf16[2,1664,256]{2,1,0:T(8,128)(2,1)S(1)} %get-tuple-element.70.qs, bf16[2,4096,256]{2,1,0:T(8,128)(2,1)S(1)} %get-tuple-element.48.ks, bf16[2,4096,256]{2,1,0:T(8,128)(2,1)S(1)} %get-tuple-element.49.vs, ...), custom_call_target="tpu_custom_call" | custom-call | flops 5200000000 | bytes 1048576 | tf_op jit(solution)/shard_map/inside2/pallas_call | solution.py:305
  26.9 0.0 collective-permute-done.5.rest_1_
  26.9 0.0 collective-permute-done.6.rest_2_
  26.9 0.0 collective-permute-done.4.rest_0_
  27.0 0.1 last.1
  27.0 2.8 %collective-permute-start.7 = (f32[2,128,128]{2,1,0:T(8,128)S(1)}, f32[2,128,128]{2,1,0:T(8,128)S(1)}, u32[]{:S(2)}, u32[]{:S(2)}) collective-permute-start(f32[2,128,128]{2,1,0:T(8,128)S(1)} %get-tuple-element.76.order), channel_id=1, source_target_pairs={{0,4},{4,0},{8,12},{12,8},{16,20},{20,16},{24,28},{28,24},{32,36},... | collective-permute-start | bytes 393224 | tf_op jit(solution)/shard_map/ppermute | solution.py:337
  29.8 1.2 %inside3.1 = (f32[2,384,128]{2,1,0:T(8,128)S(1)}, f32[2,384,128]{2,1,0:T(8,128)S(1)}, f32[2,384,128]{2,1,0:T(8,128)S(1)}) custom-call(bf16[2,384,256]{2,1,0:T(8,128)(2,1)S(1)} %get-tuple-element.83.qs, bf16[2,4096,256]{2,1,0:T(8,128)(2,1)S(1)} %get-tuple-element.48.ks, bf16[2,4096,256]{2,1,0:T(8,128)(2,1)S(1)} %get-tuple-element.49.vs, ...), custom_call_target="tpu_custom_call" | custom-call | flops 1200000000 | bytes 1048576 | tf_op jit(solution)/shard_map/inside3/pallas_call | solution.py:305
  31.0 0.0 collective-permute-done.7.got
  31.0 5.0 %outside.1 = (f32[8192,128]{1,0:T(8,128)}, f32[8192,128]{1,0:T(8,128)}, f32[8192,128]{1,0:T(8,128)}) custom-call(bf16[2,4096,256]{2,1,0:T(8,128)(2,1)S(1)} %get-tuple-element.48.ks, bf16[2,4096,256]{2,1,0:T(8,128)(2,1)S(1)} %get-tuple-element.49.vs, bf16[2,4096,256]{2,1,0:T(8,128)(2,1)S(1)} %get-tuple-element.50.gs, ...), custom_call_target="tpu_custom_call" | custom-call | flops 1000000000 | bytes 12582912 | tf_op jit(solution)/shard_map/outside/pallas_call | solution.py:341
  (1 shorter events, 0.0 us)
Async XLA Ops:
  7.7 2.7 %collective-permute-start = (f32[2,128,128]{2,1,0:T(8,128)S(1)}, f32[2,128,128]{2,1,0:T(8,128)S(1)}, u32[]{:S(2)}, u32[]{:S(2)}) collective-permute-start(f32[2,128,128]{2,1,0:T(8,128)S(1)} %get-tuple-element.52.order), channel_id=1, source_target_pairs={{0,4},{4,0},{8,12},{12,8},{16,20},{20,16},{24,28},{28,24},{32,36},... | collective-permute-start | bytes 393224 | tf_op jit(solution)/shard_map/ppermute | solution.py:319
  10.4 8.3 %collective-permute-start.2 = (f32[2,128,128]{2,1,0:T(8,128)S(1)}, f32[2,128,128]{2,1,0:T(8,128)S(1)}, u32[]{:S(2)}, u32[]{:S(2)}) collective-permute-start(f32[2,128,128]{2,1,0:T(8,128)S(1)} %get-tuple-element.59), channel_id=1, source_target_pairs={{0,16},{4,68},{8,24},{12,76},{16,0},{20,84},{24,8},{28,92},{32,48}... | collective-permute-start | bytes 393224 | tf_op jit(solution)/shard_map/ppermute | solution.py:329
  13.5 5.3 %collective-permute-start.3 = (f32[2,128,128]{2,1,0:T(8,128)S(1)}, f32[2,128,128]{2,1,0:T(8,128)S(1)}, u32[]{:S(2)}, u32[]{:S(2)}) collective-permute-start(f32[2,128,128]{2,1,0:T(8,128)S(1)} %get-tuple-element.60), channel_id=1, source_target_pairs={{0,24},{4,100},{8,16},{12,108},{16,8},{20,116},{24,0},{28,124},{32... | collective-permute-start | bytes 393224 | tf_op jit(solution)/shard_map/ppermute | solution.py:329
  14.3 4.5 %collective-permute-start.1 = (f32[2,128,128]{2,1,0:T(8,128)S(1)}, f32[2,128,128]{2,1,0:T(8,128)S(1)}, u32[]{:S(2)}, u32[]{:S(2)}) collective-permute-start(f32[2,128,128]{2,1,0:T(8,128)S(1)} %get-tuple-element.58.order.chip), channel_id=1, source_target_pairs={{0,8},{4,36},{8,0},{12,44},{16,24},{20,52},{24,16},{28,60},{32,40}... | collective-permute-start | bytes 393224 | tf_op jit(solution)/shard_map/ppermute | solution.py:329
  18.9 8.0 %collective-permute-start.5 = (f32[2,128,128]{2,1,0:T(8,128)S(1)}, f32[2,128,128]{2,1,0:T(8,128)S(1)}, u32[]{:S(2)}, u32[]{:S(2)}) collective-permute-start(f32[2,128,128]{2,1,0:T(8,128)S(1)} %get-tuple-element.68), channel_id=1, source_target_pairs={{0,64},{4,20},{8,72},{12,28},{16,80},{20,4},{24,88},{28,12},{32,96... | collective-permute-start | bytes 393224 | tf_op jit(solution)/shard_map/ppermute | solution.py:329
  21.7 5.3 %collective-permute-start.6 = (f32[2,128,128]{2,1,0:T(8,128)S(1)}, f32[2,128,128]{2,1,0:T(8,128)S(1)}, u32[]{:S(2)}, u32[]{:S(2)}) collective-permute-start(f32[2,128,128]{2,1,0:T(8,128)S(1)} %get-tuple-element.69), channel_id=1, source_target_pairs={{0,96},{4,28},{8,104},{12,20},{16,112},{20,12},{24,120},{28,4},{32... | collective-permute-start | bytes 393224 | tf_op jit(solution)/shard_map/ppermute | solution.py:329
  22.5 4.4 %collective-permute-start.4 = (f32[2,128,128]{2,1,0:T(8,128)S(1)}, f32[2,128,128]{2,1,0:T(8,128)S(1)}, u32[]{:S(2)}, u32[]{:S(2)}) collective-permute-start(f32[2,128,128]{2,1,0:T(8,128)S(1)} %get-tuple-element.67.order), channel_id=1, source_target_pairs={{0,32},{4,12},{8,40},{12,4},{16,48},{20,28},{24,56},{28,20},{32,0}... | collective-permute-start | bytes 393224 | tf_op jit(solution)/shard_map/ppermute | solution.py:329
  27.0 4.0 %collective-permute-start.7 = (f32[2,128,128]{2,1,0:T(8,128)S(1)}, f32[2,128,128]{2,1,0:T(8,128)S(1)}, u32[]{:S(2)}, u32[]{:S(2)}) collective-permute-start(f32[2,128,128]{2,1,0:T(8,128)S(1)} %get-tuple-element.76.order), channel_id=1, source_target_pairs={{0,4},{4,0},{8,12},{12,8},{16,20},{20,16},{24,28},{28,24},{32,36},... | collective-permute-start | bytes 393224 | tf_op jit(solution)/shard_map/ppermute | solution.py:337

commit v4 on v3

--- a/solution.py
+++ b/solution.py
@@ -11,7 +11,7 @@
 HEAD = 128
 HEADS = 2
 CHUNK = 128
-CUTS = (3, 13, 13, 3)
+CUTS = (2, 14, 14, 2)
 LEAD = 4
 PIECE = 5
 SLICES = len(CUTS)

time: 36.4 us -> 36.1 us (level)
    ppermute x1, starting transfers between devices: 2.78 us -> 2.4 us  [body(): got = lax.ppermute(message, 'seq', sibling)]
  transfers between devices with their start and end apart: 8 -> 8, of which waited for: 1 -> 2; matrix products, arithmetic and copies ran while one was open for 0% -> 0% of each run, Pallas kernels for 31% -> 31%
where the time goes in v4:
time: 36.1 us; the launch traced here: 36 us
  Pallas kernels  23.5 us (65%)
  starting transfers between devices  11.4 us (32%)
  between operations  0.9 us (2%)
    pallas_call x4, Pallas kernels, inside(): pl.pallas_call(functools.partial(inside_kernel, firsts[at], n), out_shape...  11.3 us
    ppermute x6, starting transfers between devices, swap(): out.append(lax.ppermute(m, 'seq', pairs))  7.54 us
    pallas_call x1, Pallas kernels, body(): pl.pallas_call(functools.partial(states_kernel, tile), out_shape=shapes,...  7.03 us
    pallas_call x1, Pallas kernels, body(): pl.pallas_call(outside_kernel, out_shape=[pltpu.HBM((tokens * HEADS, HEAD...  5.03 us
    ppermute x1, starting transfers between devices, body(): got = lax.ppermute(message, 'seq', sibling)  2.4 us
    ppermute x1, starting transfers between devices, body(): got = lax.ppermute(other, 'seq', sibling)  1.5 us
  transfers between devices with their start and end apart: 8, of which 2 were waited for; matrix products, arithmetic and copies ran while one was open for 0% of the time, Pallas kernels for 31%

profile of v4, /device:TPU:1, one launch (start us, length us, event | category | flops | bytes accessed | tf_op | source)
XLA Modules:
  0.0 36.0 jit_solution(8778351664280087682)
XLA Ops:
  0.6 7.0 %states.1 = (bf16[2,4096,256]{2,1,0:T(8,128)(2,1)S(1)}, bf16[2,4096,256]{2,1,0:T(8,128)(2,1)S(1)}, bf16[2,4096,256]{2,1,0:T(8,128)(2,1)S(1)}, f32[2,128,128]{2,1...) custom-call(f32[8192,128]{1,0:T(8,128)} %bitcast.7, ...), custom_call_target="tpu_custom_call" | custom-call | flops 1000000000 | bytes 16777216 | tf_op jit(solution)/shard_map/states/pallas_call | solution.py:277
  7.7 1.5 %collective-permute-start = (f32[2,128,128]{2,1,0:T(8,128)S(1)}, f32[2,128,128]{2,1,0:T(8,128)S(1)}, u32[]{:S(2)}, u32[]{:S(2)}) collective-permute-start(f32[2,128,128]{2,1,0:T(8,128)S(1)} %get-tuple-element.52.order), channel_id=1, source_target_pairs={{0,4},{4,0},{8,12},{12,8},{16,20},{20,16},{24,28},{28,24},{32,36},... | collective-permute-start | bytes 393224 | tf_op jit(solution)/shard_map/ppermute | solution.py:319
  9.2 0.9 %inside0.1 = (f32[2,256,128]{2,1,0:T(8,128)S(1)}, f32[2,256,128]{2,1,0:T(8,128)S(1)}, f32[2,256,128]{2,1,0:T(8,128)S(1)}) custom-call(bf16[2,256,256]{2,1,0:T(8,128)(2,1)S(1)} %get-tuple-element.53.qs, bf16[2,4096,256]{2,1,0:T(8,128)(2,1)S(1)} %get-tuple-element.48.ks, bf16[2,4096,256]{2,1,0:T(8,128)(2,1)S(1)} %get-tuple-element.49.vs, ...), custom_call_target="tpu_custom_call" | custom-call | flops 800000000 | bytes 1048576 | tf_op jit(solution)/shard_map/inside0/pallas_call | solution.py:305
  10.1 0.1 collective-permute-done.got
  10.2 3.1 %collective-permute-start.2 = (f32[2,128,128]{2,1,0:T(8,128)S(1)}, f32[2,128,128]{2,1,0:T(8,128)S(1)}, u32[]{:S(2)}, u32[]{:S(2)}) collective-permute-start(f32[2,128,128]{2,1,0:T(8,128)S(1)} %get-tuple-element.59), channel_id=1, source_target_pairs={{0,16},{4,68},{8,24},{12,76},{16,0},{20,84},{24,8},{28,92},{32,48}... | collective-permute-start | bytes 393224 | tf_op jit(solution)/shard_map/ppermute | solution.py:329
  13.3 0.8 %collective-permute-start.3 = (f32[2,128,128]{2,1,0:T(8,128)S(1)}, f32[2,128,128]{2,1,0:T(8,128)S(1)}, u32[]{:S(2)}, u32[]{:S(2)}) collective-permute-start(f32[2,128,128]{2,1,0:T(8,128)S(1)} %get-tuple-element.60), channel_id=1, source_target_pairs={{0,24},{4,100},{8,16},{12,108},{16,8},{20,116},{24,0},{28,124},{32... | collective-permute-start | bytes 393224 | tf_op jit(solution)/shard_map/ppermute | solution.py:329
  14.0 0.0 collective-permute-start.1
  14.0 4.7 %inside1.1 = (f32[2,1792,128]{2,1,0:T(8,128)S(1)}, f32[2,1792,128]{2,1,0:T(8,128)S(1)}, f32[2,1792,128]{2,1,0:T(8,128)S(1)}) custom-call(bf16[2,1792,256]{2,1,0:T(8,128)(2,1)S(1)} %get-tuple-element.61.qs, bf16[2,4096,256]{2,1,0:T(8,128)(2,1)S(1)} %get-tuple-element.48.ks, bf16[2,4096,256]{2,1,0:T(8,128)(2,1)S(1)} %get-tuple-element.49.vs, ...), custom_call_target="tpu_custom_call" | custom-call | flops 5600000000 | bytes 1048576 | tf_op jit(solution)/shard_map/inside1/pallas_call | solution.py:305
  18.8 0.0 collective-permute-done.2.rest_1_
  18.8 0.0 collective-permute-done.3.rest_2_
  18.8 0.0 collective-permute-done.1.rest_0_
  18.8 0.1 middle.1
  18.9 2.8 %collective-permute-start.5 = (f32[2,128,128]{2,1,0:T(8,128)S(1)}, f32[2,128,128]{2,1,0:T(8,128)S(1)}, u32[]{:S(2)}, u32[]{:S(2)}) collective-permute-start(f32[2,128,128]{2,1,0:T(8,128)S(1)} %get-tuple-element.68), channel_id=1, source_target_pairs={{0,64},{4,20},{8,72},{12,28},{16,80},{20,4},{24,88},{28,12},{32,96... | collective-permute-start | bytes 393224 | tf_op jit(solution)/shard_map/ppermute | solution.py:329
  21.7 0.9 %collective-permute-start.6 = (f32[2,128,128]{2,1,0:T(8,128)S(1)}, f32[2,128,128]{2,1,0:T(8,128)S(1)}, u32[]{:S(2)}, u32[]{:S(2)}) collective-permute-start(f32[2,128,128]{2,1,0:T(8,128)S(1)} %get-tuple-element.69), channel_id=1, source_target_pairs={{0,96},{4,28},{8,104},{12,20},{16,112},{20,12},{24,120},{28,4},{32... | collective-permute-start | bytes 393224 | tf_op jit(solution)/shard_map/ppermute | solution.py:329
  22.6 0.0 collective-permute-start.4
  22.6 4.7 %inside2.1 = (f32[2,1792,128]{2,1,0:T(8,128)S(1)}, f32[2,1792,128]{2,1,0:T(8,128)S(1)}, f32[2,1792,128]{2,1,0:T(8,128)S(1)}) custom-call(bf16[2,1792,256]{2,1,0:T(8,128)(2,1)S(1)} %get-tuple-element.70.qs, bf16[2,4096,256]{2,1,0:T(8,128)(2,1)S(1)} %get-tuple-element.48.ks, bf16[2,4096,256]{2,1,0:T(8,128)(2,1)S(1)} %get-tuple-element.49.vs, ...), custom_call_target="tpu_custom_call" | custom-call | flops 5600000000 | bytes 1048576 | tf_op jit(solution)/shard_map/inside2/pallas_call | solution.py:305
  27.3 0.0 collective-permute-done.5.rest_1_
  27.3 0.0 collective-permute-done.6.rest_2_
  27.3 0.0 collective-permute-done.4.rest_0_
  27.3 0.1 last.1
  27.4 2.4 %collective-permute-start.7 = (f32[2,128,128]{2,1,0:T(8,128)S(1)}, f32[2,128,128]{2,1,0:T(8,128)S(1)}, u32[]{:S(2)}, u32[]{:S(2)}) collective-permute-start(f32[2,128,128]{2,1,0:T(8,128)S(1)} %get-tuple-element.76.order), channel_id=1, source_target_pairs={{0,4},{4,0},{8,12},{12,8},{16,20},{20,16},{24,28},{28,24},{32,36},... | collective-permute-start | bytes 393224 | tf_op jit(solution)/shard_map/ppermute | solution.py:337
  29.8 0.9 %inside3.1 = (f32[2,256,128]{2,1,0:T(8,128)S(1)}, f32[2,256,128]{2,1,0:T(8,128)S(1)}, f32[2,256,128]{2,1,0:T(8,128)S(1)}) custom-call(bf16[2,256,256]{2,1,0:T(8,128)(2,1)S(1)} %get-tuple-element.83.qs, bf16[2,4096,256]{2,1,0:T(8,128)(2,1)S(1)} %get-tuple-element.48.ks, bf16[2,4096,256]{2,1,0:T(8,128)(2,1)S(1)} %get-tuple-element.49.vs, ...), custom_call_target="tpu_custom_call" | custom-call | flops 800000000 | bytes 1048576 | tf_op jit(solution)/shard_map/inside3/pallas_call | solution.py:305
  30.7 0.1 collective-permute-done.7.got
  30.8 5.0 %outside.1 = (f32[8192,128]{1,0:T(8,128)}, f32[8192,128]{1,0:T(8,128)}, f32[8192,128]{1,0:T(8,128)}) custom-call(bf16[2,4096,256]{2,1,0:T(8,128)(2,1)S(1)} %get-tuple-element.48.ks, bf16[2,4096,256]{2,1,0:T(8,128)(2,1)S(1)} %get-tuple-element.49.vs, bf16[2,4096,256]{2,1,0:T(8,128)(2,1)S(1)} %get-tuple-element.50.gs, ...), custom_call_target="tpu_custom_call" | custom-call | flops 1000000000 | bytes 12582912 | tf_op jit(solution)/shard_map/outside/pallas_call | solution.py:341
  (1 shorter events, 0.0 us)
Async XLA Ops:
  7.7 2.5 %collective-permute-start = (f32[2,128,128]{2,1,0:T(8,128)S(1)}, f32[2,128,128]{2,1,0:T(8,128)S(1)}, u32[]{:S(2)}, u32[]{:S(2)}) collective-permute-start(f32[2,128,128]{2,1,0:T(8,128)S(1)} %get-tuple-element.52.order), channel_id=1, source_target_pairs={{0,4},{4,0},{8,12},{12,8},{16,20},{20,16},{24,28},{28,24},{32,36},... | collective-permute-start | bytes 393224 | tf_op jit(solution)/shard_map/ppermute | solution.py:319
  10.2 8.6 %collective-permute-start.2 = (f32[2,128,128]{2,1,0:T(8,128)S(1)}, f32[2,128,128]{2,1,0:T(8,128)S(1)}, u32[]{:S(2)}, u32[]{:S(2)}) collective-permute-start(f32[2,128,128]{2,1,0:T(8,128)S(1)} %get-tuple-element.59), channel_id=1, source_target_pairs={{0,16},{4,68},{8,24},{12,76},{16,0},{20,84},{24,8},{28,92},{32,48}... | collective-permute-start | bytes 393224 | tf_op jit(solution)/shard_map/ppermute | solution.py:329
  13.3 5.5 %collective-permute-start.3 = (f32[2,128,128]{2,1,0:T(8,128)S(1)}, f32[2,128,128]{2,1,0:T(8,128)S(1)}, u32[]{:S(2)}, u32[]{:S(2)}) collective-permute-start(f32[2,128,128]{2,1,0:T(8,128)S(1)} %get-tuple-element.60), channel_id=1, source_target_pairs={{0,24},{4,100},{8,16},{12,108},{16,8},{20,116},{24,0},{28,124},{32... | collective-permute-start | bytes 393224 | tf_op jit(solution)/shard_map/ppermute | solution.py:329
  14.0 4.8 %collective-permute-start.1 = (f32[2,128,128]{2,1,0:T(8,128)S(1)}, f32[2,128,128]{2,1,0:T(8,128)S(1)}, u32[]{:S(2)}, u32[]{:S(2)}) collective-permute-start(f32[2,128,128]{2,1,0:T(8,128)S(1)} %get-tuple-element.58.order.chip), channel_id=1, source_target_pairs={{0,8},{4,36},{8,0},{12,44},{16,24},{20,52},{24,16},{28,60},{32,40}... | collective-permute-start | bytes 393224 | tf_op jit(solution)/shard_map/ppermute | solution.py:329
  18.9 8.4 %collective-permute-start.5 = (f32[2,128,128]{2,1,0:T(8,128)S(1)}, f32[2,128,128]{2,1,0:T(8,128)S(1)}, u32[]{:S(2)}, u32[]{:S(2)}) collective-permute-start(f32[2,128,128]{2,1,0:T(8,128)S(1)} %get-tuple-element.68), channel_id=1, source_target_pairs={{0,64},{4,20},{8,72},{12,28},{16,80},{20,4},{24,88},{28,12},{32,96... | collective-permute-start | bytes 393224 | tf_op jit(solution)/shard_map/ppermute | solution.py:329
  21.7 5.6 %collective-permute-start.6 = (f32[2,128,128]{2,1,0:T(8,128)S(1)}, f32[2,128,128]{2,1,0:T(8,128)S(1)}, u32[]{:S(2)}, u32[]{:S(2)}) collective-permute-start(f32[2,128,128]{2,1,0:T(8,128)S(1)} %get-tuple-element.69), channel_id=1, source_target_pairs={{0,96},{4,28},{8,104},{12,20},{16,112},{20,12},{24,120},{28,4},{32... | collective-permute-start | bytes 393224 | tf_op jit(solution)/shard_map/ppermute | solution.py:329
  22.6 4.8 %collective-permute-start.4 = (f32[2,128,128]{2,1,0:T(8,128)S(1)}, f32[2,128,128]{2,1,0:T(8,128)S(1)}, u32[]{:S(2)}, u32[]{:S(2)}) collective-permute-start(f32[2,128,128]{2,1,0:T(8,128)S(1)} %get-tuple-element.67.order), channel_id=1, source_target_pairs={{0,32},{4,12},{8,40},{12,4},{16,48},{20,28},{24,56},{28,20},{32,0}... | collective-permute-start | bytes 393224 | tf_op jit(solution)/shard_map/ppermute | solution.py:329
  27.4 3.4 %collective-permute-start.7 = (f32[2,128,128]{2,1,0:T(8,128)S(1)}, f32[2,128,128]{2,1,0:T(8,128)S(1)}, u32[]{:S(2)}, u32[]{:S(2)}) collective-permute-start(f32[2,128,128]{2,1,0:T(8,128)S(1)} %get-tuple-element.76.order), channel_id=1, source_target_pairs={{0,4},{4,0},{8,12},{12,8},{16,20},{20,16},{24,28},{28,24},{32,36},... | collective-permute-start | bytes 393224 | tf_op jit(solution)/shard_map/ppermute | solution.py:337

commit v5 on v4

--- a/solution.py
+++ b/solution.py
@@ -96,9 +96,9 @@
         for c in fetch(step):
             c.wait()
         back = steps - 1 - step
-        for h in range(HEADS):
-            p, s = own[0, h], own[1, h]
-            for c in range(per):
+        for c in range(per):
+            for h in range(HEADS):
+                p, s = own[0, h], own[1, h]
                 n = step * per + c
                 tok = slice(n * CHUNK, (n + 1) * CHUNK)
                 inside = pl.ds(c * CHUNK * HEADS + h, CHUNK, HEADS)
@@ -123,8 +123,8 @@
                 sg[i][m, h] = jnp.concatenate([shi, slo], axis=1)
                 sgt[i][m, h] = jnp.concatenate([shi.T, slo.T], axis=1)
                 s = s + gram(qhi, qlo, gg)
-            own[0, h] = p
-            own[1, h] = s
+                own[0, h] = p
+                own[1, h] = s
     mine[...] = own[core]
     other[...] = own[1 - core]
 

time: 36.1 us -> 36 us (level)
  no operation moved by 1% of the time
where the time goes in v5:
time: 36 us; the launch traced here: 35.9 us
  Pallas kernels  23.4 us (65%)
  starting transfers between devices  11.4 us (32%)
  between operations  0.9 us (2%)
    pallas_call x4, Pallas kernels, inside(): pl.pallas_call(functools.partial(inside_kernel, firsts[at], n), out_shape...  11.3 us
    ppermute x6, starting transfers between devices, swap(): out.append(lax.ppermute(m, 'seq', pairs))  7.54 us
    pallas_call x1, Pallas kernels, body(): pl.pallas_call(functools.partial(states_kernel, tile), out_shape=shapes,...  6.92 us
    pallas_call x1, Pallas kernels, body(): pl.pallas_call(outside_kernel, out_shape=[pltpu.HBM((tokens * HEADS, HEAD...  5.03 us
    ppermute x1, starting transfers between devices, body(): got = lax.ppermute(message, 'seq', sibling)  2.41 us
    ppermute x1, starting transfers between devices, body(): got = lax.ppermute(other, 'seq', sibling)  1.49 us
  transfers between devices with their start and end apart: 8, of which 2 were waited for; matrix products, arithmetic and copies ran while one was open for 0% of the time, Pallas kernels for 31%

profile of v5, /device:TPU:1, one launch (start us, length us, event | category | flops | bytes accessed | tf_op | source)
XLA Modules:
  0.0 35.9 jit_solution(3888783978099293193)
XLA Ops:
  0.6 6.9 %states.1 = (bf16[2,4096,256]{2,1,0:T(8,128)(2,1)S(1)}, bf16[2,4096,256]{2,1,0:T(8,128)(2,1)S(1)}, bf16[2,4096,256]{2,1,0:T(8,128)(2,1)S(1)}, f32[2,128,128]{2,1...) custom-call(f32[8192,128]{1,0:T(8,128)} %bitcast.7, ...), custom_call_target="tpu_custom_call" | custom-call | flops 1000000000 | bytes 16777216 | tf_op jit(solution)/shard_map/states/pallas_call | solution.py:277
  7.6 1.5 %collective-permute-start = (f32[2,128,128]{2,1,0:T(8,128)S(1)}, f32[2,128,128]{2,1,0:T(8,128)S(1)}, u32[]{:S(2)}, u32[]{:S(2)}) collective-permute-start(f32[2,128,128]{2,1,0:T(8,128)S(1)} %get-tuple-element.52.order), channel_id=1, source_target_pairs={{0,4},{4,0},{8,12},{12,8},{16,20},{20,16},{24,28},{28,24},{32,36},... | collective-permute-start | bytes 393224 | tf_op jit(solution)/shard_map/ppermute | solution.py:319
  9.0 0.9 %inside0.1 = (f32[2,256,128]{2,1,0:T(8,128)S(1)}, f32[2,256,128]{2,1,0:T(8,128)S(1)}, f32[2,256,128]{2,1,0:T(8,128)S(1)}) custom-call(bf16[2,256,256]{2,1,0:T(8,128)(2,1)S(1)} %get-tuple-element.53.qs, bf16[2,4096,256]{2,1,0:T(8,128)(2,1)S(1)} %get-tuple-element.48.ks, bf16[2,4096,256]{2,1,0:T(8,128)(2,1)S(1)} %get-tuple-element.49.vs, ...), custom_call_target="tpu_custom_call" | custom-call | flops 800000000 | bytes 1048576 | tf_op jit(solution)/shard_map/inside0/pallas_call | solution.py:305
  10.0 0.1 collective-permute-done.got
  10.1 3.1 %collective-permute-start.2 = (f32[2,128,128]{2,1,0:T(8,128)S(1)}, f32[2,128,128]{2,1,0:T(8,128)S(1)}, u32[]{:S(2)}, u32[]{:S(2)}) collective-permute-start(f32[2,128,128]{2,1,0:T(8,128)S(1)} %get-tuple-element.59), channel_id=1, source_target_pairs={{0,16},{4,68},{8,24},{12,76},{16,0},{20,84},{24,8},{28,92},{32,48}... | collective-permute-start | bytes 393224 | tf_op jit(solution)/shard_map/ppermute | solution.py:329
  13.1 0.8 %collective-permute-start.3 = (f32[2,128,128]{2,1,0:T(8,128)S(1)}, f32[2,128,128]{2,1,0:T(8,128)S(1)}, u32[]{:S(2)}, u32[]{:S(2)}) collective-permute-start(f32[2,128,128]{2,1,0:T(8,128)S(1)} %get-tuple-element.60), channel_id=1, source_target_pairs={{0,24},{4,100},{8,16},{12,108},{16,8},{20,116},{24,0},{28,124},{32... | collective-permute-start | bytes 393224 | tf_op jit(solution)/shard_map/ppermute | solution.py:329
  13.9 0.0 collective-permute-start.1
  13.9 4.7 %inside1.1 = (f32[2,1792,128]{2,1,0:T(8,128)S(1)}, f32[2,1792,128]{2,1,0:T(8,128)S(1)}, f32[2,1792,128]{2,1,0:T(8,128)S(1)}) custom-call(bf16[2,1792,256]{2,1,0:T(8,128)(2,1)S(1)} %get-tuple-element.61.qs, bf16[2,4096,256]{2,1,0:T(8,128)(2,1)S(1)} %get-tuple-element.48.ks, bf16[2,4096,256]{2,1,0:T(8,128)(2,1)S(1)} %get-tuple-element.49.vs, ...), custom_call_target="tpu_custom_call" | custom-call | flops 5600000000 | bytes 1048576 | tf_op jit(solution)/shard_map/inside1/pallas_call | solution.py:305
  18.6 0.0 collective-permute-done.2.rest_1_
  18.7 0.0 collective-permute-done.3.rest_2_
  18.7 0.0 collective-permute-done.1.rest_0_
  18.7 0.1 middle.1
  18.8 2.8 %collective-permute-start.5 = (f32[2,128,128]{2,1,0:T(8,128)S(1)}, f32[2,128,128]{2,1,0:T(8,128)S(1)}, u32[]{:S(2)}, u32[]{:S(2)}) collective-permute-start(f32[2,128,128]{2,1,0:T(8,128)S(1)} %get-tuple-element.68), channel_id=1, source_target_pairs={{0,64},{4,20},{8,72},{12,28},{16,80},{20,4},{24,88},{28,12},{32,96... | collective-permute-start | bytes 393224 | tf_op jit(solution)/shard_map/ppermute | solution.py:329
  21.6 0.9 %collective-permute-start.6 = (f32[2,128,128]{2,1,0:T(8,128)S(1)}, f32[2,128,128]{2,1,0:T(8,128)S(1)}, u32[]{:S(2)}, u32[]{:S(2)}) collective-permute-start(f32[2,128,128]{2,1,0:T(8,128)S(1)} %get-tuple-element.69), channel_id=1, source_target_pairs={{0,96},{4,28},{8,104},{12,20},{16,112},{20,12},{24,120},{28,4},{32... | collective-permute-start | bytes 393224 | tf_op jit(solution)/shard_map/ppermute | solution.py:329
  22.5 0.0 collective-permute-start.4
  22.5 4.7 %inside2.1 = (f32[2,1792,128]{2,1,0:T(8,128)S(1)}, f32[2,1792,128]{2,1,0:T(8,128)S(1)}, f32[2,1792,128]{2,1,0:T(8,128)S(1)}) custom-call(bf16[2,1792,256]{2,1,0:T(8,128)(2,1)S(1)} %get-tuple-element.70.qs, bf16[2,4096,256]{2,1,0:T(8,128)(2,1)S(1)} %get-tuple-element.48.ks, bf16[2,4096,256]{2,1,0:T(8,128)(2,1)S(1)} %get-tuple-element.49.vs, ...), custom_call_target="tpu_custom_call" | custom-call | flops 5600000000 | bytes 1048576 | tf_op jit(solution)/shard_map/inside2/pallas_call | solution.py:305
  27.2 0.0 collective-permute-done.5.rest_1_
  27.2 0.0 collective-permute-done.6.rest_2_
  27.2 0.0 collective-permute-done.4.rest_0_
  27.2 0.1 last.1
  27.3 2.4 %collective-permute-start.7 = (f32[2,128,128]{2,1,0:T(8,128)S(1)}, f32[2,128,128]{2,1,0:T(8,128)S(1)}, u32[]{:S(2)}, u32[]{:S(2)}) collective-permute-start(f32[2,128,128]{2,1,0:T(8,128)S(1)} %get-tuple-element.76.order), channel_id=1, source_target_pairs={{0,4},{4,0},{8,12},{12,8},{16,20},{20,16},{24,28},{28,24},{32,36},... | collective-permute-start | bytes 393224 | tf_op jit(solution)/shard_map/ppermute | solution.py:337
  29.7 0.9 %inside3.1 = (f32[2,256,128]{2,1,0:T(8,128)S(1)}, f32[2,256,128]{2,1,0:T(8,128)S(1)}, f32[2,256,128]{2,1,0:T(8,128)S(1)}) custom-call(bf16[2,256,256]{2,1,0:T(8,128)(2,1)S(1)} %get-tuple-element.83.qs, bf16[2,4096,256]{2,1,0:T(8,128)(2,1)S(1)} %get-tuple-element.48.ks, bf16[2,4096,256]{2,1,0:T(8,128)(2,1)S(1)} %get-tuple-element.49.vs, ...), custom_call_target="tpu_custom_call" | custom-call | flops 800000000 | bytes 1048576 | tf_op jit(solution)/shard_map/inside3/pallas_call | solution.py:305
  30.6 0.1 collective-permute-done.7.got
  30.7 5.0 %outside.1 = (f32[8192,128]{1,0:T(8,128)}, f32[8192,128]{1,0:T(8,128)}, f32[8192,128]{1,0:T(8,128)}) custom-call(bf16[2,4096,256]{2,1,0:T(8,128)(2,1)S(1)} %get-tuple-element.48.ks, bf16[2,4096,256]{2,1,0:T(8,128)(2,1)S(1)} %get-tuple-element.49.vs, bf16[2,4096,256]{2,1,0:T(8,128)(2,1)S(1)} %get-tuple-element.50.gs, ...), custom_call_target="tpu_custom_call" | custom-call | flops 1000000000 | bytes 12582912 | tf_op jit(solution)/shard_map/outside/pallas_call | solution.py:341
  (1 shorter events, 0.0 us)
Async XLA Ops:
  7.6 2.5 %collective-permute-start = (f32[2,128,128]{2,1,0:T(8,128)S(1)}, f32[2,128,128]{2,1,0:T(8,128)S(1)}, u32[]{:S(2)}, u32[]{:S(2)}) collective-permute-start(f32[2,128,128]{2,1,0:T(8,128)S(1)} %get-tuple-element.52.order), channel_id=1, source_target_pairs={{0,4},{4,0},{8,12},{12,8},{16,20},{20,16},{24,28},{28,24},{32,36},... | collective-permute-start | bytes 393224 | tf_op jit(solution)/shard_map/ppermute | solution.py:319
  10.1 8.6 %collective-permute-start.2 = (f32[2,128,128]{2,1,0:T(8,128)S(1)}, f32[2,128,128]{2,1,0:T(8,128)S(1)}, u32[]{:S(2)}, u32[]{:S(2)}) collective-permute-start(f32[2,128,128]{2,1,0:T(8,128)S(1)} %get-tuple-element.59), channel_id=1, source_target_pairs={{0,16},{4,68},{8,24},{12,76},{16,0},{20,84},{24,8},{28,92},{32,48}... | collective-permute-start | bytes 393224 | tf_op jit(solution)/shard_map/ppermute | solution.py:329
  13.1 5.5 %collective-permute-start.3 = (f32[2,128,128]{2,1,0:T(8,128)S(1)}, f32[2,128,128]{2,1,0:T(8,128)S(1)}, u32[]{:S(2)}, u32[]{:S(2)}) collective-permute-start(f32[2,128,128]{2,1,0:T(8,128)S(1)} %get-tuple-element.60), channel_id=1, source_target_pairs={{0,24},{4,100},{8,16},{12,108},{16,8},{20,116},{24,0},{28,124},{32... | collective-permute-start | bytes 393224 | tf_op jit(solution)/shard_map/ppermute | solution.py:329
  13.9 4.8 %collective-permute-start.1 = (f32[2,128,128]{2,1,0:T(8,128)S(1)}, f32[2,128,128]{2,1,0:T(8,128)S(1)}, u32[]{:S(2)}, u32[]{:S(2)}) collective-permute-start(f32[2,128,128]{2,1,0:T(8,128)S(1)} %get-tuple-element.58.order.chip), channel_id=1, source_target_pairs={{0,8},{4,36},{8,0},{12,44},{16,24},{20,52},{24,16},{28,60},{32,40}... | collective-permute-start | bytes 393224 | tf_op jit(solution)/shard_map/ppermute | solution.py:329
  18.8 8.4 %collective-permute-start.5 = (f32[2,128,128]{2,1,0:T(8,128)S(1)}, f32[2,128,128]{2,1,0:T(8,128)S(1)}, u32[]{:S(2)}, u32[]{:S(2)}) collective-permute-start(f32[2,128,128]{2,1,0:T(8,128)S(1)} %get-tuple-element.68), channel_id=1, source_target_pairs={{0,64},{4,20},{8,72},{12,28},{16,80},{20,4},{24,88},{28,12},{32,96... | collective-permute-start | bytes 393224 | tf_op jit(solution)/shard_map/ppermute | solution.py:329
  21.6 5.6 %collective-permute-start.6 = (f32[2,128,128]{2,1,0:T(8,128)S(1)}, f32[2,128,128]{2,1,0:T(8,128)S(1)}, u32[]{:S(2)}, u32[]{:S(2)}) collective-permute-start(f32[2,128,128]{2,1,0:T(8,128)S(1)} %get-tuple-element.69), channel_id=1, source_target_pairs={{0,96},{4,28},{8,104},{12,20},{16,112},{20,12},{24,120},{28,4},{32... | collective-permute-start | bytes 393224 | tf_op jit(solution)/shard_map/ppermute | solution.py:329
  22.5 4.8 %collective-permute-start.4 = (f32[2,128,128]{2,1,0:T(8,128)S(1)}, f32[2,128,128]{2,1,0:T(8,128)S(1)}, u32[]{:S(2)}, u32[]{:S(2)}) collective-permute-start(f32[2,128,128]{2,1,0:T(8,128)S(1)} %get-tuple-element.67.order), channel_id=1, source_target_pairs={{0,32},{4,12},{8,40},{12,4},{16,48},{20,28},{24,56},{28,20},{32,0}... | collective-permute-start | bytes 393224 | tf_op jit(solution)/shard_map/ppermute | solution.py:329
  27.3 3.4 %collective-permute-start.7 = (f32[2,128,128]{2,1,0:T(8,128)S(1)}, f32[2,128,128]{2,1,0:T(8,128)S(1)}, u32[]{:S(2)}, u32[]{:S(2)}) collective-permute-start(f32[2,128,128]{2,1,0:T(8,128)S(1)} %get-tuple-element.76.order), channel_id=1, source_target_pairs={{0,4},{4,0},{8,12},{12,8},{16,20},{20,16},{24,28},{28,24},{32,36},... | collective-permute-start | bytes 393224 | tf_op jit(solution)/shard_map/ppermute | solution.py:337
